TPU v7x, 256 devices: a whole 4x4x8 slice. The times are simulated.
256 devices in a mesh: dp: 8 (over y, core), ctx: 32 (over z, x).
Axes of the slice: x: 4, y: 4, z: 8, core: 2. Of those that a mesh axis runs over, the one named last changes fastest.
Arguments:
- inputs: bfloat16 [8, 8192, 2048], P('dp', 'ctx'), may hold values from -6 to 6
- grad_out: bfloat16 [8, 8192, 2048], P('dp', 'ctx'), may hold values from -6 to 6
- w_first: float32 [64, 33], replicated, may hold values from -1 to 1
- b_first: float32 [64], replicated, may hold values from -4 to 4
- w_mid: float32 [64, 64], replicated, may hold values from -0.75 to 0.75
- b_mid: float32 [64], replicated, may hold values from -4 to 4
- w_last: float32 [2048, 64], replicated, may hold values from -0.75 to 0.75
- decay_rate: float32 [2048], replicated, may hold values from 0.5 to 19.2
Outputs:
- clip_first: float32 [64, 33], replicated
- clip_first_bias: float32 [64], replicated
- clip_mid: float32 [64, 64], replicated
- clip_mid_bias: float32 [64], replicated
- clip_last: float32 [2048, 64], replicated
All inputs are finite; a program needn't handle non-finite values.
Results may differ from a plain program's by a relative error of at most 0.0052.
Values may be sent and summed in bfloat16 or wider, within the bound.
A program may use at most 128 MiB of HBM per device.

v0:
```python
import math

import jax
import jax.numpy as jnp
from jax import lax
from jax.sharding import PartitionSpec as P

BANDS = 16
FB = 256


def mix(form, left, right):
    return jnp.einsum(form, left, right, preferred_element_type=jnp.float32)


def exact(form, left, right):
    return jnp.einsum(form, left, right, precision=lax.Precision.HIGHEST)


def dense(left, right):
    return jnp.dot(left, right, precision=lax.Precision.HIGHEST)


def dft_tables(rows_all, cols_all):
    twice_ids = jnp.arange(2 * rows_all, dtype=jnp.int32)[:, None]
    row_ids = jnp.arange(rows_all, dtype=jnp.int32)[None, :]
    angle_rows = math.pi * (twice_ids * row_ids % (2 * rows_all)).astype(jnp.float32) / rows_all
    col_ids = jnp.arange(cols_all, dtype=jnp.int32)
    angle_cols = (
        2.0
        * math.pi
        * (col_ids[:, None] * col_ids[None, :] % cols_all).astype(jnp.float32)
        / cols_all
    )
    return (
        jnp.cos(angle_rows).astype(jnp.bfloat16),
        (-jnp.sin(angle_rows)).astype(jnp.bfloat16),
        jnp.cos(angle_cols).astype(jnp.bfloat16),
        (-jnp.sin(angle_cols)).astype(jnp.bfloat16),
    )


def twiddle(freq_ids, col_ids, seq_len):
    angle = (
        math.pi
        * (freq_ids[:, None] * col_ids[None, :] % (2 * seq_len)).astype(jnp.float32)
        / seq_len
    )
    return (jnp.cos(angle), -jnp.sin(angle))


def section_forward(stacked_pair, tables, col_ids, seq_len):
    first_re, first_im, second_re, second_im = tables
    part_re = mix("jn,vnmc->vjmc", first_re, stacked_pair)
    part_im = mix("jn,vnmc->vjmc", first_im, stacked_pair)
    turn_re, turn_im = twiddle(jnp.arange(first_re.shape[0], dtype=jnp.int32), col_ids, seq_len)
    turn_re = turn_re[None, :, :, None]
    turn_im = turn_im[None, :, :, None]
    out_re = part_re * turn_re - part_im * turn_im
    out_im = part_re * turn_im + part_im * turn_re
    stacked = jnp.stack([out_re, out_im], axis=1)
    return stacked.reshape((4,) + out_re.shape[1:]).astype(jnp.bfloat16)


def section_cross(spectra, tables, freq_ids, seq_len):
    first_re, first_im, second_re, second_im = tables
    with_re = mix("kn,sjnc->sjkc", second_re, spectra)
    with_im = mix("kn,sjnc->sjkc", second_im, spectra)
    input_re = with_re[0] - with_im[1]
    input_im = with_re[1] + with_im[0]
    grad_re = with_re[2] - with_im[3]
    grad_im = with_re[3] + with_im[2]
    cross = jnp.stack(
        [input_re * grad_re + input_im * grad_im, input_re * grad_im - input_im * grad_re]
    ).astype(jnp.bfloat16)
    back_re = mix("tk,sjkc->sjtc", second_re, cross)
    back_im = mix("tk,sjkc->sjtc", second_im, cross)
    inner_re = back_re[0] + back_im[1]
    inner_im = back_re[1] - back_im[0]
    turn_re, turn_im = twiddle(freq_ids, jnp.arange(second_re.shape[0], dtype=jnp.int32), seq_len)
    turn_re = turn_re[:, :, None]
    turn_im = turn_im[:, :, None]
    out_re = inner_re * turn_re + inner_im * turn_im
    out_im = inner_im * turn_re - inner_re * turn_im
    return jnp.stack([out_re, out_im]).astype(jnp.bfloat16)


def section_inverse(returned, tables, seq_len):
    first_re, first_im, second_re, second_im = tables
    summed = mix("jt,jmc->tmc", first_re, returned[0]) + mix("jt,jmc->tmc", first_im, returned[1])
    return summed * (0.5 / seq_len)


def features_of(places, seq_len, bands):
    band_ids = jnp.arange(1, bands + 1, dtype=jnp.int32)[:, None]
    angle = 2.0 * math.pi * (band_ids * places[None, :] % seq_len).astype(jnp.float32) / seq_len
    ramp = places[None, :].astype(jnp.float32) / seq_len
    return jnp.concatenate([ramp, jnp.cos(angle), jnp.sin(angle)], axis=0)


def hidden_forward(places, seq_len, bands, w_first, b_first, w_mid, b_mid):
    feats = features_of(places, seq_len, bands)
    pre_first = dense(w_first, feats) + b_first[:, None]
    act_first = jnp.sin(pre_first)
    pre_second = dense(w_mid, act_first) + b_mid[:, None]
    act_second = jnp.sin(pre_second)
    return (feats, pre_first, act_first, pre_second, act_second)


def hidden_backward(d_second, feats, pre_first, act_first, pre_second, w_mid):
    d_pre_second = d_second * jnp.cos(pre_second)
    grad_mid = dense(d_pre_second, act_first.T)
    grad_mid_bias = jnp.sum(d_pre_second, axis=1)
    d_pre_first = dense(w_mid.T, d_pre_second) * jnp.cos(pre_first)
    grad_first = dense(d_pre_first, feats.T)
    grad_first_bias = jnp.sum(d_pre_first, axis=1)
    return (grad_first, grad_first_bias, grad_mid, grad_mid_bias)


def modulation(places, rates, seq_len):
    return jnp.exp(-rates[None, :] * places[:, None].astype(jnp.float32) / seq_len)


def clip_factor(squares, param_count):
    return jnp.minimum(1.0, math.sqrt(param_count) / (jnp.sqrt(squares) + 1e-06))


def clip_all(grads):
    squares = sum((jnp.sum(item * item) for item in grads))
    factor = clip_factor(squares, sum((item.size for item in grads)))
    return tuple((item * factor for item in grads))


def on_device(inputs, grad_out, w_first, b_first, w_mid, b_mid, w_last, decay_rate):
    parts = lax.axis_size("ctx")
    index = lax.axis_index("ctx")
    seq_dev = inputs.shape[1]
    channels = inputs.shape[2]
    rows_dev = seq_dev // FB
    rows_all = rows_dev * parts
    seq_len = rows_all * FB
    tables = dft_tables(rows_all, FB)
    stacked_pair = jnp.stack([inputs[0], grad_out[0]])
    slice_width = channels // parts
    columns = lax.all_to_all(stacked_pair, "ctx", split_axis=2, concat_axis=1, tiled=True)
    blocks = columns.reshape(2, rows_all, FB, slice_width)
    spectra = section_forward(blocks, tables, jnp.arange(FB, dtype=jnp.int32), seq_len)
    returned = section_cross(spectra, tables, jnp.arange(2 * rows_all, dtype=jnp.int32), seq_len)
    filter_grad = section_inverse(returned, tables, seq_len).reshape(seq_len, slice_width)
    start = index * slice_width
    rates = lax.dynamic_slice_in_dim(decay_rate, start, slice_width, 0)
    last_rows = lax.dynamic_slice_in_dim(w_last, start, slice_width, 0)
    places = jnp.arange(seq_len, dtype=jnp.int32)
    feats, pre_first, act_first, pre_second, act_second = hidden_forward(
        places, seq_len, BANDS, w_first, b_first, w_mid, b_mid
    )
    shaped = filter_grad * modulation(places, rates, seq_len)
    last_slice = exact("tc,ot->co", shaped, act_second)
    d_rows = lax.psum_scatter(dense(shaped, last_rows), "ctx", scatter_dimension=0, tiled=True)
    own_start = index * seq_dev

    def pick_own(array):
        return lax.dynamic_slice_in_dim(array, own_start, seq_dev, 1)

    small_part = hidden_backward(
        d_rows.T,
        pick_own(feats),
        pick_own(pre_first),
        pick_own(act_first),
        pick_own(pre_second),
        w_mid,
    )
    small = lax.psum((small_part[0], small_part[1], small_part[2], small_part[3]), ("dp", "ctx"))
    last_data = lax.psum(last_slice, "dp")
    full_last = lax.all_gather(last_data, "ctx", axis=0, tiled=True)
    results = clip_all(tuple(small) + (full_last,))
    return results


def solution(mesh):
    in_specs = (P("dp", "ctx", None), P("dp", "ctx", None), P(), P(), P(), P(), P(), P())
    out_specs = (P(), P(), P(), P(), P())
    return jax.shard_map(
        on_device, mesh=mesh, in_specs=in_specs, out_specs=out_specs, check_vma=False
    )
```

profile of v0, /device:TPU:1, one launch (start us, length us, event | category | flops | bytes accessed | tf_op | source)
XLA Modules:
  0.0 476.9 jit_solution(15977390064671025307)
XLA Ops:
  7.2 4.7 copy.23
  11.8 5.9 %copy.24 = bf16[1,256,2048]{1,0,2:T(2,128)(2,1)} copy(bf16[1,256,2048]{2,1,0:T(8,128)(2,1)} %param.9) | data formatting | bytes 2097152 | tf_op args[1]
  17.8 6.7 %pad_maximum_fusion.4 = bf16[2,256,2048]{1,0,2:T(2,128)(2,1)} fusion(bf16[1,256,2048]{1,0,2:T(2,128)(2,1)} %copy.24, bf16[1,256,2048]{1,0,2:T(2,128)(2,1)S(1)} %copy.23), kind=kLoop, calls=%fused_computation.30 | loop fusion | flops 4194304 | bytes 4194304 | tf_op jit(solution)/shard_map/stack | solution.py:143
  24.5 11.9 %all-to-all-start = ((bf16[2,256,2048]{1,0,2:T(2,128)(2,1)}), bf16[2,256,2048]{1,0,2:T(2,128)(2,1)S(1)}, u32[]{:S(2)}, u32[]{:S(2)}) async-start(bf16[2,256,2048]{1,0,2:T(2,128)(2,1)} %pad_maximum_fusion.4), calls=%async_computation | async-start | bytes 4194304 | tf_op jit(solution)/shard_map/all_to_all | solution.py:145
  37.4 47.4 %all-to-all-done = bf16[2,256,2048]{1,0,2:T(2,128)(2,1)S(1)} async-done(((bf16[2,256,2048]{1,0,2:T(2,128)(2,1)}), bf16[2,256,2048]{1,0,2:T(2,128)(2,1)S(1)}, u32[]{:S(2)}, u32[]{:S(2)}) %all-to-all-start) | async-done | bytes 2097184 | tf_op jit(solution)/shard_map/all_to_all | solution.py:145
  84.8 3.3 fusion.8
  88.1 7.2 %fusion.5 = (bf16[2,1,64,256,64]{3,2,4,0,1:T(8,128)(2,1)}, bf16[2,1,64,256,64]{3,2,4,0,1:T(8,128)(2,1)}) fusion(f32[2,256,64,64]{1,3,2,0:T(8,128)S(1)} %fusion.8, f32[64,256]{1,0:T(8,128)S(1)} %get-tuple-element.36, f32[64,256]{1,0:T(8,128)S(1)} %get-tuple-element.37, bf16[2,256,32,64]{1,0,3,2:T(2,128)(2,1)S(1)} %bitcast.95), kind=kOutput, calls=%fused_computation.14 | convolution fusion | flops 151025664 | bytes 19005440 | tf_op jit(solution)/shard_map/jn,vnmc->vjmc/dot_general | solution.py:13
  95.3 7.5 %pad_maximum_fusion = bf16[2,2,64,256,64]{3,2,4,0,1:T(8,128)(2,1)} fusion(bf16[2,1,64,256,64]{3,2,4,0,1:T(8,128)(2,1)} %get-tuple-element.29, bf16[2,1,64,256,64]{3,2,4,0,1:T(8,128)(2,1)} %get-tuple-element.28), kind=kLoop, calls=%fused_computation.4 | loop fusion | flops 4194304 | bytes 16777216 | tf_op jit(solution)/shard_map/stack | solution.py:61
  102.8 11.5 %copy.27 = bf16[2,2,64,256,64]{3,4,2,1,0:T(8,128)(2,1)} copy(bf16[2,2,64,256,64]{3,2,4,0,1:T(8,128)(2,1)} %pad_maximum_fusion) | data formatting | bytes 16777216 | tf_op jit(solution)/shard_map/stack | solution.py:61
  114.2 12.5 %convolution_bitcast_fusion = f32[4,64,256,64]{2,3,1,0:T(8,128)} fusion(bf16[4,64,256,64]{2,3,1,0:T(8,128)(2,1)} %bitcast.92), kind=kOutput, calls=%fused_computation.2 | convolution fusion | flops 2148532224 | bytes 25165824 | tf_op jit(solution)/shard_map/kn,sjnc->sjkc/dot_general | solution.py:13
  126.8 9.2 %convolution_bitcast_fusion.1 = f32[4,64,256,64]{2,3,1,0:T(8,128)} fusion(bf16[4,64,256,64]{2,3,1,0:T(8,128)(2,1)S(1)} %bitcast.93), kind=kOutput, calls=%fused_computation.3 | convolution fusion | flops 2148466688 | bytes 25165824 | tf_op jit(solution)/shard_map/kn,sjnc->sjkc/dot_general | solution.py:13
  136.0 12.8 %add_convert_fusion.1 = (bf16[1,64,256,64]{2,3,1,0:T(8,128)(2,1)S(1)}, bf16[1,64,256,64]{2,3,1,0:T(8,128)(2,1)S(1)}) fusion(f32[4,64,256,64]{2,3,1,0:T(8,128)} %convolution_bitcast_fusion, f32[4,64,256,64]{2,3,1,0:T(8,128)} %convolution_bitcast_fusion.1), kind=kLoop, calls=%fused_computation.25 | loop fusion | flops 12582912 | bytes 37748736 | tf_op jit(solution)/shard_map/convert.2
  148.8 2.2 convolution_bitcast_fusion.3
  151.0 2.2 convolution_bitcast_fusion.2
  153.2 3.5 fusion.6
  161.3 3.8 fusion.22
  165.2 2.1 fusion.39
  167.3 10.1 %fusion.111 = (f32[8192,64]{0,1:T(8,128)S(1)}, f32[8192,64]{0,1:T(8,128)}) fusion(f32[64]{0:T(128)S(1)} %copy-done.6, f32[64,33]{0,1:T(8,128)S(1)} %copy-done.5, f32[16,8192]{1,0:T(8,128)S(1)} %get-tuple-element.31, f32[16,8192]{1,0:T(8,128)S(1)} %get-tuple-element.30, f32[1,8192]{1,0:T(1,128)S(1)} %convert_multiply_fusion), kind=kOutput, calls=%fused_computation.164 | convolution fusion | flops 208683008 | bytes 5284352 | tf_op jit(solution)/shard_map/dot_general | solution.py:21
  177.4 2.0 convolution_add_fusion
  181.3 8.8 %fusion.16 = f32[64,64]{1,0:T(8,128)S(1)} fusion(f32[8192,64]{0,1:T(8,128)S(1)} %convolution_add_fusion, f32[8192,64]{0,1:T(8,128)S(1)} %bitcast.97, f32[8192]{0:T(1024)S(1)} %iota_convert_fusion, f32[64]{0:T(128)S(1)} %dynamic-slice_negate_fusion), kind=kOutput, calls=%fused_computation.39 | convolution fusion | flops 404226048 | bytes 4243712 | tf_op jit(solution)/shard_map/tc,ot->co/dot_general | solution.py:17
  190.1 23.7 %psum.39 = f32[64,64]{1,0:T(8,128)S(1)} all-reduce(f32[64,64]{1,0:T(8,128)S(1)} %fusion.16), channel_id=1, replica_groups=mesh['dp'=8,'ctx'=32] {'dp'}, use_global_device_ids=true, to_apply=%region_11.12 | all-reduce | flops 4096 | bytes 32768 | tf_op jit(solution)/shard_map/psum | solution.py:174
  213.8 42.0 %all_gather.3 = f32[2048,64]{1,0:T(8,128)S(1)} all-gather(f32[64,64]{1,0:T(8,128)S(1)} %psum.39), channel_id=1, replica_groups=mesh['dp'=8,'ctx'=32] {'ctx'}, dimensions={0}, use_global_device_ids=true | all-gather | bytes 540672 | tf_op jit(solution)/shard_map/all_gather | solution.py:175
  256.7 119.0 %reduce-scatter.2.cloned.1.call-done = f32[256,64]{0,1:T(8,128)} async-done(((f32[8192,64]{0,1:T(8,128)}), f32[256,64]{0,1:T(8,128)}) %reduce-scatter.2.cloned.1.call-update) | async-done | bytes 65552 | tf_op jit(solution)/shard_map/reduce_scatter | solution.py:159
  380.7 79.9 %all-reduce = (f32[64,33]{0,1:T(8,128)S(1)}, f32[64]{0:T(128)S(1)}, f32[64,64]{1,0:T(8,128)S(1)}, f32[64]{0:T(128)S(1)}) all-reduce(f32[64,33]{0,1:T(8,128)S(1)} %fusion.57, f32[64]{0:T(128)S(1)} %get-tuple-element.34, f32[64,64]{1,0:T(8,128)S(1)} %fusion.52, f32[64]{0:T(128)S(1)} %fusion.110), channel_id=1, replica_groups=mesh['dp'=8,'ctx'=32] {'dp','ctx'}, use_global_device_ids=true, to_apply=%region_1.2 | all-reduce | flops 6336 | bytes 50688 | tf_op jit(solution)/shard_map/psum | solution.py:173
  (42 shorter events, 19.3 us)
Async XLA Ops:
  7.2 154.1 %copy-start = (f32[2048,64]{0,1:T(8,128)S(1)}, f32[2048,64]{0,1:T(8,128)}, u32[]{:S(2)}) copy-start(f32[2048,64]{0,1:T(8,128)} %param.14) | copy-start | bytes 1572868
  24.5 60.4 %all-to-all-start = ((bf16[2,256,2048]{1,0,2:T(2,128)(2,1)}), bf16[2,256,2048]{1,0,2:T(2,128)(2,1)S(1)}, u32[]{:S(2)}, u32[]{:S(2)}) async-start(bf16[2,256,2048]{1,0,2:T(2,128)(2,1)} %pad_maximum_fusion.4), calls=%async_computation | async-start | bytes 4194304 | tf_op jit(solution)/shard_map/all_to_all | solution.py:145
  36.3 339.3 %reduce-scatter.2.cloned.1.call-start = ((), (), s32[]{:S(2)}) async-start(), calls=%async_computation.2 | async-start | bytes 2162688 | tf_op jit(solution)/shard_map/reduce_scatter | solution.py:159
  114.2 12.6 %copy-start.1 = (bf16[2,2,64,256,64]{3,4,2,1,0:T(8,128)(2,1)S(1)}, bf16[2,2,64,256,64]{3,4,2,1,0:T(8,128)(2,1)}, u32[]{:S(2)}) copy-start(bf16[2,2,64,256,64]{3,4,2,1,0:T(8,128)(2,1)} %copy.27) | copy-start | bytes 25165828
  165.1 2.2 copy-start.5
  165.1 2.2 copy-start.6
  167.3 10.1 %copy-start.4 = (f32[64,64]{1,0:T(8,128)S(1)}, f32[64,64]{1,0:T(8,128)}, u32[]{:S(2)}) copy-start(f32[64,64]{1,0:T(8,128)} %param.12) | copy-start | bytes 49156
  167.3 10.1 %copy-start.7 = (f32[64]{0:T(128)S(1)}, f32[64]{0:T(128)}, u32[]{:S(2)}) copy-start(f32[64]{0:T(128)} %param.13) | copy-start | bytes 772
  177.4 2.1 copy-start.3
  179.5 1.8 copy-start.2
Sparse Core Ops, SparseCore 0:
  165.2 210.4 reduce-scatter.1
where the time goes:
time: 483 us; the launch traced here: 477 us
  waiting for transfers between devices  166 us (34%)
  blocking collectives  146 us (30%)
  matrix products  68.6 us (14%)
  other arithmetic  41.8 us (9%)
  local copies, waits for them, and re-layouts  24.8 us (5%)
  between operations  17.8 us (4%)
  starting transfers between devices  11.9 us (2%)
    reduce_scatter x1, waiting for transfers between devices, on_device(): lax.psum_scatter(dense(shaped, last_rows), 'ctx', scatter_dimension=0, ti...  119 us
    psum x1, blocking collectives, on_device(): lax.psum((small_part[0], small_part[1], small_part[2], small_part[3]), ('...  79.9 us
    all_to_all x1, waiting for transfers between devices, on_device(): lax.all_to_all(stacked_pair, 'ctx', split_axis=2, concat_axis=1, tiled=True)  47.4 us
    all_gather x1, blocking collectives, on_device(): full_last = lax.all_gather(last_data, 'ctx', axis=0, tiled=True)  42 us
    dot_general x8, matrix products, mix(): return jnp.einsum(form, left, right, preferred_element_type=jnp.float32)  40 us
    psum x1, blocking collectives, on_device(): last_data = lax.psum(last_slice, 'dp')  23.7 us
    dot_general x6, matrix products, dense(): return jnp.dot(left, right, precision=lax.Precision.HIGHEST)  19.8 us
    unnamed x20, local copies, waits for them, and re-layouts  13.3 us
  transfers between devices with their start and end apart: 2, of which 2 were waited for; matrix products, arithmetic and copies ran while one was open for 6% of the time, Pallas kernels for 0%

commit v1 on v0

--- a/solution.py
+++ b/solution.py
@@ -22,7 +22,7 @@
 
 
 def dft_tables(rows_all, cols_all):
-    twice_ids = jnp.arange(2 * rows_all, dtype=jnp.int32)[:, None]
+    twice_ids = jnp.arange(rows_all + 1, dtype=jnp.int32)[:, None]
     row_ids = jnp.arange(rows_all, dtype=jnp.int32)[None, :]
     angle_rows = math.pi * (twice_ids * row_ids % (2 * rows_all)).astype(jnp.float32) / rows_all
     col_ids = jnp.arange(cols_all, dtype=jnp.int32)
@@ -87,7 +87,11 @@
 
 def section_inverse(returned, tables, seq_len):
     first_re, first_im, second_re, second_im = tables
-    summed = mix("jt,jmc->tmc", first_re, returned[0]) + mix("jt,jmc->tmc", first_im, returned[1])
+    last = first_re.shape[0] - 1
+    twice = jnp.where((jnp.arange(last + 1) % last == 0)[:, None], 1.0, 2.0).astype(jnp.bfloat16)
+    summed = mix("jt,jmc->tmc", first_re * twice, returned[0]) + mix(
+        "jt,jmc->tmc", first_im * twice, returned[1]
+    )
     return summed * (0.5 / seq_len)
 
 
@@ -145,7 +149,7 @@
     columns = lax.all_to_all(stacked_pair, "ctx", split_axis=2, concat_axis=1, tiled=True)
     blocks = columns.reshape(2, rows_all, FB, slice_width)
     spectra = section_forward(blocks, tables, jnp.arange(FB, dtype=jnp.int32), seq_len)
-    returned = section_cross(spectra, tables, jnp.arange(2 * rows_all, dtype=jnp.int32), seq_len)
+    returned = section_cross(spectra, tables, jnp.arange(rows_all + 1, dtype=jnp.int32), seq_len)
     filter_grad = section_inverse(returned, tables, seq_len).reshape(seq_len, slice_width)
     start = index * slice_width
     rates = lax.dynamic_slice_in_dim(decay_rate, start, slice_width, 0)
@@ -156,20 +160,8 @@
     )
     shaped = filter_grad * modulation(places, rates, seq_len)
     last_slice = exact("tc,ot->co", shaped, act_second)
-    d_rows = lax.psum_scatter(dense(shaped, last_rows), "ctx", scatter_dimension=0, tiled=True)
-    own_start = index * seq_dev
-
-    def pick_own(array):
-        return lax.dynamic_slice_in_dim(array, own_start, seq_dev, 1)
-
-    small_part = hidden_backward(
-        d_rows.T,
-        pick_own(feats),
-        pick_own(pre_first),
-        pick_own(act_first),
-        pick_own(pre_second),
-        w_mid,
-    )
+    d_second = exact("co,tc->ot", last_rows, shaped)
+    small_part = hidden_backward(d_second, feats, pre_first, act_first, pre_second, w_mid)
     small = lax.psum((small_part[0], small_part[1], small_part[2], small_part[3]), ("dp", "ctx"))
     last_data = lax.psum(last_slice, "dp")
     full_last = lax.all_gather(last_data, "ctx", axis=0, tiled=True)

time: 483 us -> 305 us (0.63)
  waiting for transfers between devices: 166 us -> 30.5 us
  other arithmetic: 41.8 us -> 19.9 us
  between operations: 17.8 us -> 4.51 us
  local copies, waits for them, and re-layouts: 24.8 us -> 17.6 us
  blocking collectives: 146 us -> 151 us
  matrix products: 68.6 us -> 63.6 us
    reduce_scatter x1 -> x0, waiting for transfers between devices: 119 us -> none  [on_device(): lax.psum_scatter(dense(shaped, last_rows), 'ctx', scatter_dimension=0, ti...]
    dot_general x8, matrix products: 40 us -> 17.8 us  [mix(): return jnp.einsum(form, left, right, preferred_element_type=jnp.float32)]
    all_to_all x1, waiting for transfers between devices: 47.4 us -> 30.5 us  [on_device(): lax.all_to_all(stacked_pair, 'ctx', split_axis=2, concat_axis=1, tiled=True)]
    another operation x1, other arithmetic: 12.8 us -> 2.36 us
    another operation x1, local copies, waits for them, and re-layouts: 11.5 us -> 1.05 us  [section_forward(): stacked = jnp.stack([out_re, out_im], axis=1)]
    dot_general x1 -> x2, matrix products: 8.85 us -> 17.9 us  [exact(): return jnp.einsum(form, left, right, precision=lax.Precision.HIGHEST)]
    psum x1, blocking collectives: 79.9 us -> 88.9 us  [on_device(): lax.psum((small_part[0], small_part[1], small_part[2], small_part[3]), ('...]
    dot_general x6 -> x5, matrix products: 19.8 us -> 27.9 us  [dense(): return jnp.dot(left, right, precision=lax.Precision.HIGHEST)]
  transfers between devices with their start and end apart: 2 -> 1, of which waited for: 2 -> 1; matrix products, arithmetic and copies ran while one was open for 6% -> 6% of each run, Pallas kernels for 0% -> 0%
where the time goes in v1:
time: 305 us; the launch traced here: 299 us
  blocking collectives  151 us (50%)
  matrix products  63.6 us (21%)
  waiting for transfers between devices  30.5 us (10%)
  other arithmetic  19.9 us (7%)
  local copies, waits for them, and re-layouts  17.6 us (6%)
  starting transfers between devices  12 us (4%)
  between operations  4.51 us (1%)
    psum x1, blocking collectives, on_device(): lax.psum((small_part[0], small_part[1], small_part[2], small_part[3]), ('...  88.9 us
    all_gather x1, blocking collectives, on_device(): full_last = lax.all_gather(last_data, 'ctx', axis=0, tiled=True)  39 us
    all_to_all x1, waiting for transfers between devices, on_device(): lax.all_to_all(stacked_pair, 'ctx', split_axis=2, concat_axis=1, tiled=True)  30.5 us
    dot_general x5, matrix products, dense(): return jnp.dot(left, right, precision=lax.Precision.HIGHEST)  27.9 us
    psum x1, blocking collectives, on_device(): last_data = lax.psum(last_slice, 'dp')  23 us
    dot_general x2, matrix products, exact(): return jnp.einsum(form, left, right, precision=lax.Precision.HIGHEST)  17.9 us
    dot_general x8, matrix products, mix(): return jnp.einsum(form, left, right, preferred_element_type=jnp.float32)  17.8 us
    unnamed x34, local copies, waits for them, and re-layouts  16.6 us
  transfers between devices with their start and end apart: 1, of which 1 were waited for; matrix products, arithmetic and copies ran while one was open for 6% of the time, Pallas kernels for 0%

profile of v1, /device:TPU:1, one launch (start us, length us, event | category | flops | bytes accessed | tf_op | source)
XLA Modules:
  0.0 298.9 jit_solution(4672298125866611335)
XLA Ops:
  0.6 4.7 %copy.23 = bf16[1,256,2048]{1,0,2:T(2,128)(2,1)S(1)} copy(bf16[1,256,2048]{2,1,0:T(8,128)(2,1)} %param.8) | data formatting | bytes 2097152 | tf_op args[0]
  5.3 5.9 %copy.24 = bf16[1,256,2048]{1,0,2:T(2,128)(2,1)} copy(bf16[1,256,2048]{2,1,0:T(8,128)(2,1)} %param.9) | data formatting | bytes 2097152 | tf_op args[1]
  11.3 6.7 %pad_maximum_fusion.2 = bf16[2,256,2048]{1,0,2:T(2,128)(2,1)} fusion(bf16[1,256,2048]{1,0,2:T(2,128)(2,1)} %copy.24, bf16[1,256,2048]{1,0,2:T(2,128)(2,1)S(1)} %copy.23), kind=kLoop, calls=%fused_computation.30 | loop fusion | flops 4194304 | bytes 4194304 | tf_op jit(solution)/shard_map/stack | solution.py:147
  17.9 12.0 %all-to-all-start = ((bf16[2,256,2048]{1,0,2:T(2,128)(2,1)}), bf16[2,256,2048]{1,0,2:T(2,128)(2,1)S(1)}, u32[]{:S(2)}, u32[]{:S(2)}) async-start(bf16[2,256,2048]{1,0,2:T(2,128)(2,1)} %pad_maximum_fusion.2), calls=%async_computation | async-start | bytes 4194304 | tf_op jit(solution)/shard_map/all_to_all | solution.py:149
  31.0 2.1 fusion.36
  33.1 10.1 %fusion.108 = (f32[8192,64]{0,1:T(8,128)S(1)}, f32[8192,64]{0,1:T(8,128)}) fusion(f32[64]{0:T(128)S(1)} %copy-done.13, f32[64,33]{0,1:T(8,128)S(1)} %copy-done.12, f32[16,8192]{1,0:T(8,128)S(1)} %get-tuple-element.31, f32[16,8192]{1,0:T(8,128)S(1)} %get-tuple-element.30, f32[1,8192]{1,0:T(1,128)S(1)} %convert_multiply_fusion), kind=kOutput, calls=%fused_computation.165 | convolution fusion | flops 208683008 | bytes 5284352 | tf_op jit(solution)/shard_map/dot_general | solution.py:21
  44.6 3.4 %convolution_add_fusion = f32[8192,64]{0,1:T(8,128)} fusion(f32[8192,64]{0,1:T(8,128)S(1)} %get-tuple-element.32, f32[64,64]{1,0:T(8,128)S(1)} %copy-done.11, f32[64]{0:T(128)S(1)} %copy-done.14), kind=kOutput, calls=%fused_computation.1 | convolution fusion | flops 403177472 | bytes 4210944 | tf_op jit(solution)/shard_map/dot_general | solution.py:21
  47.9 30.5 %all-to-all-done = bf16[2,256,2048]{1,0,2:T(2,128)(2,1)S(1)} async-done(((bf16[2,256,2048]{1,0,2:T(2,128)(2,1)}), bf16[2,256,2048]{1,0,2:T(2,128)(2,1)S(1)}, u32[]{:S(2)}, u32[]{:S(2)}) %all-to-all-start) | async-done | bytes 2097184 | tf_op jit(solution)/shard_map/all_to_all | solution.py:149
  78.4 3.1 %fusion.6 = f32[2,256,64,33]{1,3,2,0:T(8,128)S(1)} fusion(bf16[2,256,32,64]{1,0,3,2:T(2,128)(2,1)S(1)} %bitcast.99), kind=kOutput, calls=%fused_computation.31 | convolution fusion | flops 69222912 | bytes 6422528 | tf_op jit(solution)/shard_map/jn,vnmc->vjmc/dot_general | solution.py:13
  81.5 4.3 %fusion.5 = (bf16[2,1,33,256,64]{3,2,4,0,1:T(8,128)(2,1)S(1)}, bf16[2,1,33,256,64]{3,2,4,0,1:T(8,128)(2,1)S(1)}) fusion(f32[2,256,64,33]{1,3,2,0:T(8,128)S(1)} %fusion.6, f32[33,256]{1,0:T(8,128)S(1)} %get-tuple-element.38, f32[33,256]{1,0:T(8,128)S(1)} %get-tuple-element.39, bf16[2,256,32,64]{1,0,3,2:T(2,128)(2,1)S(1)} %bitcast.100), kind=kOutput, calls=%fused_computation.16 | convolution fusion | flops 77872608 | bytes 10815488 | tf_op jit(solution)/shard_map/jn,vnmc->vjmc/dot_general | solution.py:13
  87.4 2.2 convolution_bitcast_fusion
  89.6 2.6 convolution_bitcast_fusion.1
  92.3 2.4 add_convert_fusion.1
  94.6 1.7 convolution_bitcast_fusion.3
  96.3 1.7 convolution_bitcast_fusion.2
  98.0 1.5 fusion.18
  104.2 9.0 %fusion.10 = f32[64,64]{1,0:T(8,128)S(1)} fusion(f32[8192,64]{0,1:T(8,128)S(1)} %copy-done.3, f32[8192,64]{0,1:T(8,128)S(1)} %bitcast.101, f32[8192]{0:T(1024)S(1)} %iota_convert_fusion, f32[64]{0:T(128)S(1)} %dynamic-slice_negate_fusion), kind=kOutput, calls=%fused_computation.35 | convolution fusion | flops 404226048 | bytes 4243712 | tf_op jit(solution)/shard_map/tc,ot->co/dot_general | solution.py:17
  113.2 23.0 %psum.39 = f32[64,64]{1,0:T(8,128)S(1)} all-reduce(f32[64,64]{1,0:T(8,128)S(1)} %fusion.10), channel_id=1, replica_groups=mesh['dp'=8,'ctx'=32] {'dp'}, use_global_device_ids=true, to_apply=%region_10.11 | all-reduce | flops 4096 | bytes 32768 | tf_op jit(solution)/shard_map/psum | solution.py:166
  136.3 39.0 %all_gather.3 = f32[2048,64]{1,0:T(8,128)S(1)} all-gather(f32[64,64]{1,0:T(8,128)S(1)} %psum.39), channel_id=1, replica_groups=mesh['dp'=8,'ctx'=32] {'ctx'}, dimensions={0}, use_global_device_ids=true | all-gather | bytes 540672 | tf_op jit(solution)/shard_map/all_gather | solution.py:167
  177.2 8.9 %fusion.110 = (f32[64]{0:T(128)S(1)}, f32[64,8192]{1,0:T(8,128)S(1)}) fusion(f32[8192,64]{0,1:T(8,128)S(1)} %copy-done.3, f32[8192,64]{0,1:T(8,128)S(1)} %bitcast.102, f32[8192]{0:T(1024)S(1)} %iota_convert_fusion, f32[64]{0:T(128)S(1)} %dynamic-slice_negate_fusion, f32[2048,64]{0,1:T(8,128)S(1)} %copy-done, s32[]{:T(128)S(6)} %select_n.96), kind=kOutput, calls=%fused_computation.167 | convolution fusion | flops 405274560 | bytes 6357764 | tf_op jit(solution)/shard_map/co,tc->ot/dot_general | solution.py:17
  186.1 1.8 fusion.115
  187.9 10.8 %fusion.109 = (f32[64]{0:T(128)S(1)}, f32[8192,64]{0,1:T(8,128)S(1)}) fusion(f32[8192,64]{0,1:T(8,128)S(1)} %copy-done.8, f32[64,8192]{1,0:T(8,128)S(1)} %get-tuple-element.37, f32[64,64]{1,0:T(8,128)S(1)} %copy-done.11), kind=kOutput, calls=%fused_computation.166 | convolution fusion | flops 403701696 | bytes 6308096 | tf_op jit(solution)/shard_map/dot_general | solution.py:21
  198.7 1.9 fusion.25
  200.6 88.9 %all-reduce = (f32[64,33]{0,1:T(8,128)S(1)}, f32[64]{0:T(128)S(1)}, f32[64,64]{1,0:T(8,128)S(1)}, f32[64]{0:T(128)S(1)}) all-reduce(f32[64,33]{0,1:T(8,128)S(1)} %fusion.25, f32[64]{0:T(128)S(1)} %get-tuple-element.34, f32[64,64]{1,0:T(8,128)S(1)} %fusion.115, f32[64]{0:T(128)S(1)} %get-tuple-element.36), channel_id=1, replica_groups=mesh['dp'=8,'ctx'=32] {'dp','ctx'}, use_global_device_ids=true, to_apply=%region_0.1 | all-reduce | flops 6336 | bytes 50688 | tf_op jit(solution)/shard_map/psum | solution.py:165
  (52 shorter events, 16.4 us)
Async XLA Ops:
  0.6 176.5 %copy-start = (f32[2048,64]{0,1:T(8,128)S(1)}, f32[2048,64]{0,1:T(8,128)}, u32[]{:S(2)}) copy-start(f32[2048,64]{0,1:T(8,128)} %param.14) | copy-start | bytes 1572868
  17.9 15.2 %copy-start.12 = (f32[64,33]{0,1:T(8,128)S(1)}, f32[64,33]{0,1:T(8,128)}, u32[]{:S(2)}) copy-start(f32[64,33]{0,1:T(8,128)} %param.10) | copy-start | bytes 25348
  17.9 15.2 %copy-start.13 = (f32[64]{0:T(128)S(1)}, f32[64]{0:T(128)}, u32[]{:S(2)}) copy-start(f32[64]{0:T(128)} %param.11) | copy-start | bytes 772
  17.9 60.5 %all-to-all-start = ((bf16[2,256,2048]{1,0,2:T(2,128)(2,1)}), bf16[2,256,2048]{1,0,2:T(2,128)(2,1)S(1)}, u32[]{:S(2)}, u32[]{:S(2)}) async-start(bf16[2,256,2048]{1,0,2:T(2,128)(2,1)} %pad_maximum_fusion.2), calls=%async_computation | async-start | bytes 4194304 | tf_op jit(solution)/shard_map/all_to_all | solution.py:149
  33.1 10.2 %copy-start.9 = (f32[16,8192]{1,0:T(8,128)}, f32[16,8192]{1,0:T(8,128)S(1)}, u32[]{:S(2)}) copy-start(f32[16,8192]{1,0:T(8,128)S(1)} %get-tuple-element.31) | copy-start | bytes 1572868
  33.1 11.4 %copy-start.11 = (f32[64,64]{1,0:T(8,128)S(1)}, f32[64,64]{1,0:T(8,128)}, u32[]{:S(2)}) copy-start(f32[64,64]{1,0:T(8,128)} %param.12) | copy-start | bytes 49156
  33.1 11.4 %copy-start.14 = (f32[64]{0:T(128)S(1)}, f32[64]{0:T(128)}, u32[]{:S(2)}) copy-start(f32[64]{0:T(128)} %param.13) | copy-start | bytes 772
  43.3 1.3 copy-start.1
  101.7 2.5 copy-start.3
  102.9 1.3 copy-start.4
  136.3 40.9 %copy-start.5 = (f32[8,8,32,256]{3,1,2,0:T(8,128)S(1)}, f32[8,8,32,256]{3,1,2,0:T(8,128)}, u32[]{:S(2)}) copy-start(f32[8,8,32,256]{3,1,2,0:T(8,128)} %copy-done.4) | copy-start | bytes 6291460
  175.2 1.0 copy-start.6
  177.2 8.9 %copy-start.2 = (f32[8192,64]{0,1:T(8,128)S(1)}, f32[8192,64]{0,1:T(8,128)}, u32[]{:S(2)}) copy-start(f32[8192,64]{0,1:T(8,128)} %copy-done.1) | copy-start | bytes 6291460
  186.1 1.8 copy-start.8
  187.9 10.8 %copy-start.10 = (f32[16,8192]{1,0:T(8,128)S(1)}, f32[16,8192]{1,0:T(8,128)}, u32[]{:S(2)}) copy-start(f32[16,8192]{1,0:T(8,128)} %copy-done.9) | copy-start | bytes 1572868
  198.7 96.5 %copy-start.7 = (f32[2048,64]{1,0:T(8,128)S(1)}, f32[2048,64]{1,0:T(8,128)}, u32[]{:S(2)}) copy-start(f32[2048,64]{1,0:T(8,128)} %copy-done.6) | copy-start | bytes 1572868

commit v2 on v1

v2 whole, which is shorter than its diff:
```python
import functools
import math

import jax
import jax.numpy as jnp
import ml_dtypes
import numpy as np
from jax import lax
from jax.experimental import pallas as pl
from jax.experimental.pallas import tpu as pltpu
from jax.sharding import PartitionSpec as P

BANDS = 16
FB = 256
CC = 16
BF = jnp.bfloat16
F32 = jnp.float32
HI = lax.Precision.HIGHEST
MESH = pl.DeviceIdType.MESH


def make_tables(rows):
    seq = rows * FB
    half = rows + 1
    j = np.arange(half, dtype=np.int64)
    n = np.arange(rows, dtype=np.int64)
    m = np.arange(FB, dtype=np.int64)
    f32, bf = np.float32, ml_dtypes.bfloat16
    ang = (f32(math.pi) * (j[:, None] * n[None, :] % (2 * rows)).astype(f32) / f32(rows)).astype(f32)
    fr = np.cos(ang).astype(bf).astype(f32)
    fi = (-np.sin(ang)).astype(bf).astype(f32)
    ang = (f32(2.0 * math.pi) * (m[:, None] * m[None, :] % FB).astype(f32) / f32(FB)).astype(f32)
    er = np.cos(ang).astype(bf).astype(f32)
    ei = (-np.sin(ang)).astype(bf).astype(f32)
    ang = (f32(math.pi) * (j[:, None] * m[None, :] % (2 * seq)).astype(f32) / f32(seq)).astype(f32)
    tw = np.stack([np.cos(ang), -np.sin(ang)]).astype(f32)
    eye = np.eye(CC, dtype=f32)
    forward = np.kron(np.concatenate([fr, fi], 0), eye).astype(bf)
    e_fwd = np.block([[er.T, ei.T], [-ei.T, er.T]]).astype(bf)
    e_inv = np.block([[er.T, -ei.T], [ei.T, er.T]]).astype(bf)
    twice = np.where(j % rows == 0, 1.0, 2.0).astype(f32)[:, None]
    both = np.concatenate([fr * twice, (fi * twice)[1:rows]], 0) * f32(0.5 / seq)
    inverse = np.kron(both.T, eye).astype(bf)
    q = np.arange(seq, dtype=np.int64)
    band = np.arange(1, BANDS + 1, dtype=np.int64)[:, None]
    ang = (f32(2.0 * math.pi) * (band * q[None, :] % seq).astype(f32) / f32(seq)).astype(f32)
    ramp = (q[None, :].astype(f32) / f32(seq)).astype(f32)
    feats = np.concatenate([ramp, np.cos(ang), np.sin(ang)], 0).astype(f32)
    return forward, e_fwd, e_inv, inverse, tw, feats


def nt(left, right):
    return lax.dot_general(left, right, (((1,), (1,)), ((), ())), preferred_element_type=F32)


def mm(left, right):
    return jnp.dot(left, right, preferred_element_type=F32)


def exact(left, right):
    return jnp.dot(left, right, precision=HI, preferred_element_type=F32)


def transform_kernel(
    parts,
    x_ref, g_ref, fwd_ref, ef_ref, ei_ref, inv_ref, tw_ref, feats_ref,
    wf_ref, bf_ref, wm_ref, wmt_ref, bm_ref, wl_ref, rate_ref,
    out_ref,
    send, recv, spec, back, act_x, cos_first, act_second, cos_second, feat_x, modul, shaped,
    send_sem, recv_sem,
):
    me = lax.axis_index("ctx")
    channels = x_ref.shape[1]
    own = channels // parts
    chunks = own // CC
    half = parts + 1
    order = feats_ref.shape[0]
    seq = feats_ref.shape[1]
    hidden = wm_ref.shape[0]

    barrier = pltpu.get_barrier_semaphore()

    @pl.loop(1, parts)
    def _(r):
        pl.semaphore_signal(
            barrier, inc=1, device_id={"ctx": lax.rem(me + r, parts)}, device_id_type=MESH
        )

    @pl.loop(0, channels // 128)
    def _(e):
        lanes = pl.ds(pl.multiple_of(e * 128, 128), 128)
        for v, ref in enumerate((x_ref, g_ref)):
            turned = ref[:, lanes].T
            for i in range(128 // own):
                for k in range(chunks):
                    row = i * own + k * CC
                    send[e * (128 // own) + i, k, v] = turned[row : row + CC]

    pl.semaphore_wait(barrier, parts - 1)
    mine = pl.ds(pl.multiple_of(me * CC, CC), CC)

    def copy_to(r, k):
        target = lax.rem(me + r, parts)
        return pltpu.make_async_remote_copy(
            src_ref=send.at[target, k],
            dst_ref=recv.at[k, :, mine],
            send_sem=send_sem.at[k],
            recv_sem=recv_sem.at[k],
            device_id={"ctx": target},
            device_id_type=MESH,
        )

    for k in range(chunks):

        @pl.loop(0, parts - 1)
        def _(i):
            step = i // 2 + 1
            r = jnp.where(lax.rem(i, 2) == 0, step, parts - step)
            copy_to(r, k).start()

    for k in range(chunks):
        recv[k, :, mine] = send[me, k]

    width = 512
    act_x[hidden:, :] = jnp.where(
        lax.broadcasted_iota(jnp.int32, (128 - hidden, seq), 0) == 34, 1.0, 0.0
    ).astype(BF)

    @pl.loop(0, seq // width)
    def _(i):
        at = pl.ds(pl.multiple_of(i * width, width), width)
        feats = feats_ref[:, at]
        pre_first = exact(wf_ref[...], feats) + bf_ref[...]
        first = jnp.sin(pre_first)
        cos_first[:, at] = jnp.cos(pre_first)
        act_x[:hidden, at] = first.astype(BF)
        pre_second = exact(wm_ref[...], first) + bm_ref[...]
        act_second[:, at] = jnp.sin(pre_second).astype(BF)
        cos_second[:, at] = jnp.cos(pre_second)
        places = (i * width + lax.broadcasted_iota(jnp.int32, (1, width), 1)).astype(F32)
        modul[:, at] = jnp.exp(-(rate_ref[...] * places) / seq)
        feat_x[:hidden, at] = jnp.zeros((hidden, width), BF)
        tail = jnp.concatenate(
            [feats, jnp.ones((1, width), F32), jnp.zeros((128 - hidden - order - 1, width), F32)], axis=0
        )
        feat_x[hidden:, at] = tail.astype(BF)

    @pl.loop(0, chunks)
    def _(k):
        for which in (send_sem, recv_sem):
            pltpu.make_async_copy(
                recv.at[k, :, : (parts - 1) * CC], recv.at[k, :, : (parts - 1) * CC], which.at[k]
            ).wait()
        turn_re = tw_ref[0][:, None, :]
        turn_im = tw_ref[1][:, None, :]
        for v in range(2):
            part = mm(fwd_ref[...], recv[k, v])
            part_re = part[: half * CC].reshape(half, CC, FB)
            part_im = part[half * CC :].reshape(half, CC, FB)
            spec[:, v, :, :FB] = (part_re * turn_re - part_im * turn_im).astype(BF)
            spec[:, v, :, FB:] = (part_re * turn_im + part_im * turn_re).astype(BF)
        both = mm(spec[...].reshape(half * 2 * CC, 2 * FB), ef_ref[...]).reshape(half, 2, CC, 2 * FB)
        x_re, x_im = both[:, 0, :, :FB], both[:, 0, :, FB:]
        g_re, g_im = both[:, 1, :, :FB], both[:, 1, :, FB:]
        cross = jnp.concatenate(
            [(x_re * g_re + x_im * g_im).astype(BF), (x_re * g_im - x_im * g_re).astype(BF)], axis=-1
        )
        inner = mm(cross.reshape(half * CC, 2 * FB), ei_ref[...]).reshape(half, CC, 2 * FB)
        in_re, in_im = inner[:, :, :FB], inner[:, :, FB:]
        back[:half] = (in_re * turn_re + in_im * turn_im).astype(BF)
        back[half:] = (in_im * turn_re - in_re * turn_im)[1:parts].astype(BF)
        grad = mm(inv_ref[...], back[...].reshape(2 * parts * CC, FB))
        rows = pl.ds(pl.multiple_of(k * CC, CC), CC)
        for s in range(parts):
            at = slice(s * FB, (s + 1) * FB)
            shaped[rows, at] = (grad[s * CC : (s + 1) * CC] * modul[rows, at]).astype(BF)

    span = 1024
    wl = wl_ref[...].astype(BF)
    wmt = wmt_ref[...].astype(BF)

    def step(i, carry):
        last, small = carry
        at = pl.ds(pl.multiple_of(i * span, span), span)
        sh = shaped[:, at]
        last = last + nt(act_second[:, at], sh)
        d_second = (mm(wl, sh) * cos_second[:, at]).astype(BF)
        d_first = (mm(wmt, d_second) * cos_first[:, at]).astype(BF)
        small = small + nt(d_second, act_x[:, at]) + nt(d_first, feat_x[:, at])
        return last, small

    last, small = lax.fori_loop(
        0, seq // span, step, (jnp.zeros((hidden, own), F32), jnp.zeros((hidden, 128), F32))
    )
    last = jnp.concatenate([last, jnp.zeros((hidden, 128 - own), F32)], axis=1)
    odd = lax.rem(me, 2) == 1
    last = jnp.where(odd, pltpu.roll(last, own, 1), last)
    groups = out_ref.shape[0]
    out_ref[:, : hidden // groups] = last.reshape(groups, hidden // groups, 128)
    out_ref[:, hidden // groups :] = small.reshape(groups, hidden // groups, 128)


def reduce_kernel(
    groups, parts, count,
    part_ref,
    last_ref, mid_ref, turned_ref, factor_ref,
    got, own, ring, fin, small,
    sems,
):
    dp = lax.axis_index("dp")
    ctx = lax.axis_index("ctx")
    rows = part_ref.shape[1] // 2

    barrier = pltpu.get_barrier_semaphore()

    @pl.loop(1, parts)
    def _(r):
        pl.semaphore_signal(
            barrier, inc=1, device_id={"ctx": lax.rem(ctx + r, parts)}, device_id_type=MESH
        )

    @pl.loop(1, groups)
    def _(r):
        pl.semaphore_signal(
            barrier, inc=1, device_id={"dp": lax.rem(dp + r, groups)}, device_id_type=MESH
        )

    pl.semaphore_wait(barrier, parts + groups - 2)

    def wait(ref, send, recv):
        for which in (send, recv):
            pltpu.make_async_copy(ref, ref, sems.at[which]).wait()

    @pl.loop(1, groups)
    def _(r):
        target = lax.rem(dp + r, groups)
        pltpu.make_async_remote_copy(
            src_ref=part_ref.at[target], dst_ref=got.at[groups - r],
            send_sem=sems.at[0], recv_sem=sems.at[1],
            device_id={"dp": target}, device_id_type=MESH,
        ).start()

    wait(got.at[1:groups], 0, 1)
    total = part_ref[dp]
    for r in range(1, groups):
        total = total + got[r]
    own[...] = total
    ring[0] = total

    @pl.loop(1, parts)
    def _(r):
        target = lax.rem(ctx + r, parts)
        pltpu.make_async_remote_copy(
            src_ref=own, dst_ref=ring.at[parts - r],
            send_sem=sems.at[2], recv_sem=sems.at[3],
            device_id={"ctx": target}, device_id_type=MESH,
        ).start()

    wait(ring.at[1:parts], 2, 3)
    low = lax.broadcasted_iota(jnp.int32, (rows, 128), 1) < 64
    summed = jnp.zeros((rows, 128), F32)
    for e in range(parts // 2):
        first = ring[lax.rem(2 * e + parts - ctx, parts)]
        second = ring[lax.rem(2 * e + 1 + parts - ctx, parts)]
        fin[dp, :, 128 * e : 128 * (e + 1)] = jnp.where(low, first[:rows], second[:rows]).astype(BF)
        summed = summed + first[rows:] + second[rows:]
    small[dp] = summed

    @pl.loop(1, groups)
    def _(r):
        target = lax.rem(dp + r, groups)
        for ref, base in ((fin, 4), (small, 6)):
            pltpu.make_async_remote_copy(
                src_ref=ref.at[dp], dst_ref=ref.at[dp],
                send_sem=sems.at[base], recv_sem=sems.at[base + 1],
                device_id={"dp": target}, device_id_type=MESH,
            ).start()

    wait(fin.at[: groups - 1], 4, 5)
    wait(small.at[: groups - 1], 6, 7)
    grads = fin[...].astype(F32)
    others = small[...].reshape(groups * rows, 128)
    squares = jnp.sum(jnp.sum(grads * grads, axis=0), keepdims=True) + jnp.sum(others * others, keepdims=True)
    factor = jnp.minimum(1.0, math.sqrt(count) / (jnp.sqrt(squares) + 1e-06))
    last_ref[...] = fin[...]
    mid_ref[...] = others * factor
    turned_ref[...] = (others * factor).T
    factor_ref[...] = jnp.broadcast_to(factor, (8, 128))


def on_device(inputs, grad_out, w_first, b_first, w_mid, b_mid, w_last, decay_rate):
    parts = lax.axis_size("ctx")
    groups = lax.axis_size("dp")
    index = lax.axis_index("ctx")
    channels = inputs.shape[2]
    hidden, order = w_first.shape
    own = channels // parts
    chunks = own // CC
    half = parts + 1
    seq = parts * FB
    tables = make_tables(parts)
    w_own = lax.dynamic_slice_in_dim(w_last.T, index * own, own, 1)
    rates = lax.dynamic_slice_in_dim(decay_rate, index * own, own, 0)
    vmem = pl.BlockSpec(memory_space=pltpu.VMEM)
    part = pl.pallas_call(
        functools.partial(transform_kernel, parts),
        out_shape=jax.ShapeDtypeStruct((groups, 2 * hidden // groups, 128), F32),
        in_specs=[vmem] * 15,
        out_specs=vmem,
        scratch_shapes=[
            pltpu.VMEM((parts, chunks, 2, CC, FB), BF),
            pltpu.VMEM((chunks, 2, parts * CC, FB), BF),
            pltpu.VMEM((half, 2, CC, 2 * FB), BF),
            pltpu.VMEM((2 * parts, CC, FB), BF),
            pltpu.VMEM((128, seq), BF),
            pltpu.VMEM((hidden, seq), F32),
            pltpu.VMEM((hidden, seq), BF),
            pltpu.VMEM((hidden, seq), F32),
            pltpu.VMEM((128, seq), BF),
            pltpu.VMEM((own, seq), F32),
            pltpu.VMEM((own, seq), BF),
            pltpu.SemaphoreType.DMA((chunks,)),
            pltpu.SemaphoreType.DMA((chunks,)),
        ],
        compiler_params=pltpu.CompilerParams(
            collective_id=0, has_side_effects=True, vmem_limit_bytes=60 * 1024 * 1024
        ),
    )(
        inputs[0], grad_out[0], *tables,
        w_first, b_first[:, None], w_mid, w_mid.T, b_mid[:, None], w_own, rates[:, None],
    )
    count = hidden * (order + hidden + 2) + channels * hidden
    last, mid, turned, factor = pl.pallas_call(
        functools.partial(reduce_kernel, groups, parts, count),
        out_shape=(
            jax.ShapeDtypeStruct((groups, hidden // groups, channels), BF),
            jax.ShapeDtypeStruct((hidden, 128), F32),
            jax.ShapeDtypeStruct((128, hidden), F32),
            jax.ShapeDtypeStruct((8, 128), F32),
        ),
        in_specs=[vmem],
        out_specs=(vmem,) * 4,
        scratch_shapes=[
            pltpu.VMEM((groups, 2 * hidden // groups, 128), F32),
            pltpu.VMEM((2 * hidden // groups, 128), F32),
            pltpu.VMEM((parts, 2 * hidden // groups, 128), F32),
            pltpu.VMEM((groups, hidden // groups, channels), BF),
            pltpu.VMEM((groups, hidden // groups, 128), F32),
            pltpu.SemaphoreType.DMA((8,)),
        ],
        compiler_params=pltpu.CompilerParams(
            collective_id=1, has_side_effects=True, vmem_limit_bytes=32 * 1024 * 1024
        ),
    )(part)
    clip_last = (last.reshape(hidden, channels).astype(F32) * factor[0, 0]).T
    clip_first = turned[hidden : hidden + order].T
    return (clip_first, turned[hidden + order], mid[:, :hidden], turned[hidden + order + 1], clip_last)


def solution(mesh):
    in_specs = (P("dp", "ctx", None), P("dp", "ctx", None), P(), P(), P(), P(), P(), P())
    out_specs = (P(), P(), P(), P(), P())
    return jax.shard_map(
        on_device, mesh=mesh, in_specs=in_specs, out_specs=out_specs, check_vma=False
    )
```

time: 305 us -> 107 us (0.35); the launches traced: 299 us -> 106 us
  blocking collectives: 151 us -> 0 us
  Pallas kernels: 0 us -> 93 us
  matrix products: 63.6 us -> 0 us
  waiting for transfers between devices: 30.5 us -> 0 us
  other arithmetic: 19.9 us -> 1.48 us
  starting transfers between devices: 12 us -> 0 us
  local copies, waits for them, and re-layouts: 17.6 us -> 11.1 us
  between operations: 4.51 us -> 0.67 us
    psum x2 -> x0, blocking collectives: 112 us -> none  [the longest x1 88.9 us: on_device(): lax.psum((small_part[0], small_part[1], small_part[2], small_part[3]), ('...]
    pallas_call x0 -> x2, Pallas kernels: none -> 93 us  [the longest x1 65.6 us: on_device(): pl.pallas_call(functools.partial(transform_kernel, parts), out_shape=jax....]
    dot_general x15 -> x0, matrix products: 63.6 us -> none  [the longest x5 27.9 us: dense(): return jnp.dot(left, right, precision=lax.Precision.HIGHEST)]
    all_gather x1 -> x0, blocking collectives: 39 us -> none  [on_device(): full_last = lax.all_gather(last_data, 'ctx', axis=0, tiled=True)]
    all_to_all x1 -> x0, waiting for transfers between devices: 30.5 us -> none  [on_device(): lax.all_to_all(stacked_pair, 'ctx', split_axis=2, concat_axis=1, tiled=True)]
    unnamed x34 -> x7, local copies, waits for them, and re-layouts: 16.6 us -> 4.54 us
    all_to_all x1 -> x0, starting transfers between devices: 12 us -> none  [on_device(): lax.all_to_all(stacked_pair, 'ctx', split_axis=2, concat_axis=1, tiled=True)]
    another operation x3 -> x0, other arithmetic: 9.54 us -> none  [the longest x1 6.68 us: on_device(): stacked_pair = jnp.stack([inputs[0], grad_out[0]])]
  transfers between devices with their start and end apart: 1 -> 0, of which waited for: 1 -> 0; matrix products, arithmetic and copies ran while one was open for 6% -> 0% of each run, Pallas kernels for 0% -> 0%
where the time goes in v2:
time: 107 us; the launch traced here: 106 us
  Pallas kernels  93 us (87%)
  local copies, waits for them, and re-layouts  11.1 us (10%)
  other arithmetic  1.48 us (1%)
    pallas_call x1, Pallas kernels, on_device(): pl.pallas_call(functools.partial(transform_kernel, parts), out_shape=jax....  65.6 us
    pallas_call x1, Pallas kernels, on_device(): pl.pallas_call(functools.partial(reduce_kernel, groups, parts, count), ou...  27.4 us
    unnamed x7, local copies, waits for them, and re-layouts  4.54 us

profile of v2, /device:TPU:1, one launch (start us, length us, event | category | flops | bytes accessed | tf_op | source)
XLA Modules:
  0.0 106.2 jit_solution(11210991453676420187)
XLA Ops:
  0.6 0.0 copy-start
  0.7 0.8 dynamic-slice_bitcast_fusion.1
  1.5 0.2 copy-done
  1.7 0.7 dynamic-slice_bitcast_fusion.wl_ref
  2.4 0.7 copy.23.rate_ref
  3.1 1.4 %copy.20.wf_ref = f32[64,33]{1,0:T(8,128)} copy(f32[64,33]{0,1:T(8,128)} %param.16) | data formatting | bytes 16896 | tf_op args[2]
  4.5 1.4 %copy.21.bf_ref = f32[64,1]{1,0:T(8,128)} copy(f32[64,1]{0,1:T(1,128)} %bitcast.25) | data formatting | bytes 512 | tf_op jit(solution)/shard_map/broadcast_in_dim | solution.py:330
  5.9 1.4 %copy.22.bm_ref = f32[64,1]{1,0:T(8,128)} copy(f32[64,1]{0,1:T(1,128)} %bitcast.26) | data formatting | bytes 512 | tf_op jit(solution)/shard_map/broadcast_in_dim | solution.py:330
  7.2 1.4 %copy.19 = f32[64,64]{0,1:T(8,128)} copy(f32[64,64]{1,0:T(8,128)} %wm_ref.1) | data formatting | bytes 32768 | tf_op args[4]
  8.6 65.6 %shard_map.173.part_ref = f32[8,16,128]{2,1,0:T(8,128)} custom-call(bf16[256,2048]{1,0:T(8,128)(2,1)} %bitcast.22, bf16[256,2048]{1,0:T(8,128)(2,1)} %bitcast.23, bf16[1056,512]{1,0:T(8,128)(2,1)} %constant.22.clone.fwd_ref, bf16[512,512]{1,0:T(8,128)(2,1)} %constant.23.clone.ef_ref, bf16[512,512]{1,0:T(8,128)(2,1)} %constant.24.clone.ei_ref, ...), custom_call_target="tpu_custom_call" | custom-call | tf_op jit(solution)/shard_map/pallas_call | solution.py:305
  74.3 0.0 copy-start.1
  74.3 0.8 copy-done.1
  75.1 27.4 %shard_map.174 = (bf16[8,8,2048]{2,1,0:T(8,128)(2,1)S(1)}, f32[64,128]{1,0:T(8,128)S(1)}, f32[128,64]{1,0:T(8,128)S(1)}, f32[8,128]{1,0:T(8,128)S(1)}) custom-call(f32[8,16,128]{2,1,0:T(8,128)S(1)} %copy-done.1), custom_call_target="tpu_custom_call" | custom-call | tf_op jit(solution)/shard_map/pallas_call | solution.py:333
  102.5 0.5 slice.19
  103.0 0.5 slice_bitcast_fusion.1
  103.5 0.6 slice_bitcast_fusion
  104.1 1.5 %multiply_bitcast_fusion = f32[2048,64]{0,1:T(8,128)} fusion(bf16[8,8,2048]{2,1,0:T(8,128)(2,1)S(1)} %get-tuple-element.11, f32[]{:T(128)} %bitcast.10), kind=kLoop, calls=%fused_computation | loop fusion | flops 262144 | bytes 786436 | tf_op jit(solution)/shard_map/transpose | solution.py:355
  105.6 0.6 copy.25
Async XLA Ops:
  0.6 1.1 %copy-start = (f32[2048,64]{0,1:T(8,128)S(1)}, f32[2048,64]{0,1:T(8,128)}, u32[]{:S(2)}) copy-start(f32[2048,64]{0,1:T(8,128)} %param.20) | copy-start | bytes 1572868
  74.3 0.8 copy-start.1

commit v3 on v2

v3 whole, which is shorter than its diff:
```python
import functools
import math

import jax
import jax.numpy as jnp
import ml_dtypes
import numpy as np
from jax import lax
from jax.experimental import pallas as pl
from jax.experimental.pallas import tpu as pltpu
from jax.sharding import PartitionSpec as P

BANDS = 16
FB = 256
CC = 16
BF = jnp.bfloat16
F32 = jnp.float32
MESH = pl.DeviceIdType.MESH
FP = 48
SPAN = 2048
PI_HIGH = 1.570770263671875
PI_LOW = math.pi / 2 - PI_HIGH


def make_tables(rows):
    seq = rows * FB
    half = rows + 1
    j = np.arange(half, dtype=np.int64)
    n = np.arange(rows, dtype=np.int64)
    m = np.arange(FB, dtype=np.int64)
    f32, bf = np.float32, ml_dtypes.bfloat16
    ang = (f32(math.pi) * (j[:, None] * n[None, :] % (2 * rows)).astype(f32) / f32(rows)).astype(f32)
    fr = np.cos(ang).astype(bf).astype(f32)
    fi = (-np.sin(ang)).astype(bf).astype(f32)
    ang = (f32(2.0 * math.pi) * (m[:, None] * m[None, :] % FB).astype(f32) / f32(FB)).astype(f32)
    er = np.cos(ang).astype(bf).astype(f32)
    ei = (-np.sin(ang)).astype(bf).astype(f32)
    ang = (f32(math.pi) * (j[:, None] * m[None, :] % (2 * seq)).astype(f32) / f32(seq)).astype(f32)
    tw = np.stack([np.cos(ang), -np.sin(ang)]).astype(f32)
    eye = np.eye(CC, dtype=f32)
    forward = np.kron(np.concatenate([fr, fi], 0), eye).astype(bf)
    e_fwd = np.block([[er.T, ei.T], [-ei.T, er.T]]).astype(bf)
    e_inv = np.block([[er.T, -ei.T], [ei.T, er.T]]).astype(bf)
    twice = np.where(j % rows == 0, 1.0, 2.0).astype(f32)[:, None]
    both = np.concatenate([fr * twice, (fi * twice)[1:rows]], 0) * f32(0.5 / seq)
    inverse = np.kron(both.T, eye).astype(bf)
    q = np.arange(seq, dtype=np.int64)
    band = np.arange(1, BANDS + 1, dtype=np.int64)[:, None]
    ang = (f32(2.0 * math.pi) * (band * q[None, :] % seq).astype(f32) / f32(seq)).astype(f32)
    ramp = (q[None, :].astype(f32) / f32(seq)).astype(f32)
    feats = np.concatenate([ramp, np.cos(ang), np.sin(ang)], 0).astype(f32)
    high = feats.astype(bf)
    low = (feats - high.astype(f32)).astype(bf)
    zero = np.zeros((FP - feats.shape[0], seq), bf)
    ones = zero.copy()
    ones[0] = 1
    stack = np.concatenate([high, ones, low, zero], 0)
    return forward, e_fwd, e_inv, inverse, tw, stack


def nt(left, right):
    return lax.dot_general(left, right, (((1,), (1,)), ((), ())), preferred_element_type=F32)


def mm(left, right):
    return jnp.dot(left, right, preferred_element_type=F32)


def halves(value):
    high = value.astype(BF).astype(F32)
    return high, value - high


def column(row):
    n = row.shape[1]
    on = lax.broadcasted_iota(jnp.int32, (n, n), 0) == lax.broadcasted_iota(jnp.int32, (n, n), 1)
    return jnp.sum(jnp.where(on, jnp.broadcast_to(row, (n, n)), 0.0), axis=1, keepdims=True)


def sin_cos(value):
    turns = jnp.floor(value * (2.0 / math.pi) + 0.5)
    rest = (value - turns * PI_HIGH) - turns * PI_LOW
    square = rest * rest
    sine = rest + rest * square * (
        -1.6666654611e-1 + square * (8.3321608736e-3 + square * -1.9515295891e-4)
    )
    cosine = (1.0 - 0.5 * square) + square * square * (
        4.166664568298827e-2 + square * (-1.388731625493765e-3 + square * 2.443315711809948e-5)
    )
    quarter = turns.astype(jnp.int32)
    swap = (quarter & 1) == 1
    first = jnp.where(swap, cosine, sine)
    second = jnp.where(swap, sine, cosine)
    return (
        jnp.where((quarter & 2) == 2, -first, first),
        jnp.where(((quarter + 1) & 2) == 2, -second, second),
    )


def main_kernel(
    parts, groups,
    x_any, g_any, fwd_any, ef_any, ei_any, inv_any, tw_any, feats_any, wl_any,
    wf_ref, bf_ref, wm_ref, bm_ref, rate_ref,
    last_ref, small_ref,
    x_ref, g_ref, fwd_ref, ef_ref, ei_ref, inv_ref, tw_ref, feats_ref, wl_ref,
    send, recv, spec, back, cos_first, act_second, cos_second, wide, modul,
    part, got, own_part, ring, fin, small,
    load_sem, send_sem, recv_sem, sems,
):
    ctx = lax.axis_index("ctx")
    dp = lax.axis_index("dp")
    channels = x_ref.shape[1]
    own = channels // parts
    chunks = own // CC
    half = parts + 1
    order, hidden = wf_ref.shape
    seq = cos_first.shape[1]
    pair = 128 // own

    lanes_own = pl.ds(pl.multiple_of((ctx // pair) * 128, 128), 128)
    loads = [
        pltpu.make_async_copy(source, target, load_sem.at[i])
        for i, (source, target) in enumerate(
            (
                (x_any, x_ref), (g_any, g_ref), (wl_any.at[:, lanes_own], wl_ref), (feats_any, feats_ref),
                (tw_any, tw_ref), (fwd_any, fwd_ref), (ef_any, ef_ref), (ei_any, ei_ref), (inv_any, inv_ref),
            )
        )
    ]
    for load in loads:
        load.start()

    barrier = pltpu.get_barrier_semaphore()

    @pl.loop(1, parts)
    def _(r):
        pl.semaphore_signal(
            barrier, inc=1, device_id={"ctx": lax.rem(ctx + r, parts)}, device_id_type=MESH
        )

    @pl.loop(1, groups)
    def _(r):
        pl.semaphore_signal(
            barrier, inc=1, device_id={"dp": lax.rem(dp + r, groups)}, device_id_type=MESH
        )

    mine = pl.ds(pl.multiple_of(ctx * CC, CC), CC)

    def copy_to(target, k):
        return pltpu.make_async_remote_copy(
            src_ref=send.at[target, k],
            dst_ref=recv.at[k, :, mine],
            send_sem=send_sem.at[k],
            recv_sem=recv_sem.at[k],
            device_id={"ctx": target},
            device_id_type=MESH,
        )

    loads[0].wait()
    loads[1].wait()
    pl.semaphore_wait(barrier, parts + groups - 2)

    @pl.loop(0, channels // 128)
    def _(i):
        e = lax.rem(ctx // pair + i + 1, channels // 128)
        lanes = pl.ds(pl.multiple_of(e * 128, 128), 128)
        for v, ref in enumerate((x_ref, g_ref)):
            turned = ref[:, lanes].T
            for a in range(pair):
                for k in range(chunks):
                    row = a * own + k * CC
                    send[e * pair + a, k, v] = turned[row : row + CC]
        for a in range(pair):

            @pl.when(e * pair + a != ctx)
            def _():
                copy_to(e * pair + a, 0).start()

    for k in range(1, chunks):

        @pl.loop(0, parts - 1)
        def _(i):
            step = i // 2 + 1
            r = jnp.where(lax.rem(i, 2) == 0, step, parts - step)
            copy_to(lax.rem(ctx + r, parts), k).start()

    for k in range(chunks):
        recv[k, :, mine] = send[ctx, k]

    for load in loads[2:]:
        load.wait()
    width = 512
    top = 256 - own
    wf = jnp.concatenate([wf_ref[...], jnp.zeros((FP - order, hidden), F32)], axis=0)
    wf_high, wf_low = halves(wf)
    wf_stack = jnp.concatenate([wf_high, wf_high, wf_low], axis=0).T.astype(BF)
    wm_high, wm_low = halves(wm_ref[...])
    wm_stack = jnp.concatenate([wm_high.T, wm_high.T, wm_low.T], axis=0).T.astype(BF)
    first_bias = column(bf_ref[...].reshape(1, hidden))
    second_bias = column(bm_ref[...].reshape(1, hidden))
    odd = lax.rem(ctx, pair) == 1
    rates = rate_ref[lanes_own].reshape(1, 128)
    rates = jnp.where(odd, pltpu.roll(jnp.broadcast_to(rates, (8, 128)), own, 1)[:1], rates)
    decay = column(rates[:, :own])
    wide[hidden : hidden + FP] = feats_ref[:FP]
    wide[hidden + FP : 128] = jnp.zeros((128 - hidden - FP, seq), BF)
    wide[128 : 128 + FP] = feats_ref[FP:]
    wide[128 + FP : top] = jnp.zeros((top - 128 - FP, seq), BF)

    @pl.loop(0, seq // width)
    def _(i):
        at = pl.ds(pl.multiple_of(i * width, width), width)
        high = feats_ref[:FP, at]
        stack = jnp.concatenate([high, feats_ref[FP:, at], high], axis=0)
        first, cos_one = sin_cos(mm(wf_stack, stack) + first_bias)
        cos_first[:, at] = cos_one
        high, low = halves(first)
        high, low = high.astype(BF), low.astype(BF)
        wide[:hidden, at] = high
        stack = jnp.concatenate([high, low, high], axis=0)
        second, cos_two = sin_cos(mm(wm_stack, stack) + second_bias)
        act_second[:, at] = second.astype(BF)
        cos_second[:, at] = cos_two
        places = (i * width + lax.broadcasted_iota(jnp.int32, (1, width), 1)).astype(F32)
        modul[:, at] = jnp.exp(-(decay * places) / seq)

    @pl.loop(0, chunks)
    def _(k):
        for which in (send_sem, recv_sem):
            pltpu.make_async_copy(
                recv.at[k, :, : (parts - 1) * CC], recv.at[k, :, : (parts - 1) * CC], which.at[k]
            ).wait()
        turn_re = tw_ref[0][:, None, :]
        turn_im = tw_ref[1][:, None, :]
        for v in range(2):
            part_all = mm(fwd_ref[...], recv[k, v])
            part_re = part_all[: half * CC].reshape(half, CC, FB)
            part_im = part_all[half * CC :].reshape(half, CC, FB)
            spec[:, v, :, :FB] = (part_re * turn_re - part_im * turn_im).astype(BF)
            spec[:, v, :, FB:] = (part_re * turn_im + part_im * turn_re).astype(BF)
        both = mm(spec[...].reshape(half * 2 * CC, 2 * FB), ef_ref[...]).reshape(half, 2, CC, 2 * FB)
        x_re, x_im = both[:, 0, :, :FB], both[:, 0, :, FB:]
        g_re, g_im = both[:, 1, :, :FB], both[:, 1, :, FB:]
        cross = jnp.concatenate(
            [(x_re * g_re + x_im * g_im).astype(BF), (x_re * g_im - x_im * g_re).astype(BF)], axis=-1
        )
        inner = mm(cross.reshape(half * CC, 2 * FB), ei_ref[...]).reshape(half, CC, 2 * FB)
        in_re, in_im = inner[:, :, :FB], inner[:, :, FB:]
        back[:half] = (in_re * turn_re + in_im * turn_im).astype(BF)
        back[half:] = (in_im * turn_re - in_re * turn_im)[1:parts].astype(BF)
        grad = mm(inv_ref[...], back[...].reshape(2 * parts * CC, FB))
        first_row = pl.multiple_of(k * CC, CC)
        for s in range(parts):
            at = slice(s * FB, (s + 1) * FB)
            wide[pl.ds(top + first_row, CC), at] = (
                grad[s * CC : (s + 1) * CC] * modul[pl.ds(first_row, CC), at]
            ).astype(BF)

    span = SPAN
    tile = jnp.where(odd, pltpu.roll(wl_ref[...], own, 1), wl_ref[...])[:, :own]
    high, low = halves(tile.T)
    wl_stack = jnp.concatenate([high, low], axis=0).T.astype(BF)
    wmt_stack = jnp.concatenate([wm_high, wm_low], axis=0).T.astype(BF)
    total = jnp.zeros((3 * hidden, 256), F32)
    for i in range(seq // span):
        at = slice(i * span, (i + 1) * span)
        sh = wide[top:, at]
        d_second = (mm(wl_stack, jnp.concatenate([sh, sh], axis=0)) * cos_second[:, at]).astype(BF)
        d_first = (
            mm(wmt_stack, jnp.concatenate([d_second, d_second], axis=0)) * cos_first[:, at]
        ).astype(BF)
        lines = jnp.concatenate([d_second, d_first, act_second[:, at]], axis=0)
        total = total + nt(lines, wide[:, at])

    rows = hidden // groups
    lane = lax.broadcasted_iota(jnp.int32, (hidden, 128), 1)
    by_second, by_first = total[:hidden], total[hidden : 2 * hidden]
    at_bias = hidden + order
    mixed = by_first[:, :128] + pltpu.roll(by_first[:, 128:], hidden, 1)
    mixed = jnp.where(lane < hidden, by_second[:, :128], mixed)
    mixed = jnp.where(lane == at_bias + 1, pltpu.roll(by_second[:, :128], 1, 1), mixed)
    mixed = jnp.where(lane > at_bias + 1, 0.0, mixed)
    last = total[2 * hidden :, 128:]
    last = jnp.where(odd, last, pltpu.roll(last, own, 1))
    part[:, :rows] = last.reshape(groups, rows, 128)
    part[:, rows:] = mixed.reshape(groups, rows, 128)

    def wait(ref, first, second):
        for which in (first, second):
            pltpu.make_async_copy(ref, ref, sems.at[which]).wait()

    @pl.loop(1, groups)
    def _(r):
        target = lax.rem(dp + r, groups)
        pltpu.make_async_remote_copy(
            src_ref=part.at[target], dst_ref=got.at[groups - r],
            send_sem=sems.at[0], recv_sem=sems.at[1],
            device_id={"dp": target}, device_id_type=MESH,
        ).start()

    wait(got.at[1:groups], 0, 1)
    summed = part[dp]
    for r in range(1, groups):
        summed = summed + got[r]
    own_part[...] = summed
    ring[0] = summed

    @pl.loop(1, parts)
    def _(r):
        target = lax.rem(ctx + r, parts)
        pltpu.make_async_remote_copy(
            src_ref=own_part, dst_ref=ring.at[parts - r],
            send_sem=sems.at[2], recv_sem=sems.at[3],
            device_id={"ctx": target}, device_id_type=MESH,
        ).start()

    wait(ring.at[1:parts], 2, 3)
    low_lanes = lax.broadcasted_iota(jnp.int32, (rows, 128), 1) < own
    summed = jnp.zeros((rows, 128), F32)
    for e in range(parts // 2):
        one = ring[lax.rem(2 * e + parts - ctx, parts)]
        two = ring[lax.rem(2 * e + 1 + parts - ctx, parts)]
        fin[dp, :, 128 * e : 128 * (e + 1)] = jnp.where(low_lanes, one[:rows], two[:rows]).astype(BF)
        summed = summed + one[rows:] + two[rows:]
    small[dp] = summed

    @pl.loop(1, groups)
    def _(r):
        target = lax.rem(dp + r, groups)
        for ref, base in ((fin, 4), (small, 6)):
            pltpu.make_async_remote_copy(
                src_ref=ref.at[dp], dst_ref=ref.at[dp],
                send_sem=sems.at[base], recv_sem=sems.at[base + 1],
                device_id={"dp": target}, device_id_type=MESH,
            ).start()

    wait(fin.at[: groups - 1], 4, 5)
    wait(small.at[: groups - 1], 6, 7)
    last_ref[...] = fin[...]
    small_ref[...] = small[...]


def clip_kernel(count, last_in, small_in, first_ref, first_bias_ref, mid_ref, mid_bias_ref, last_ref):
    groups, rows, channels = last_in.shape
    hidden = groups * rows
    order = first_ref.shape[0]
    grads = last_in[...].astype(F32)
    others = small_in[...].reshape(hidden, 128)
    squares = jnp.sum(jnp.sum(grads * grads, axis=0), keepdims=True) + jnp.sum(others * others, keepdims=True)
    factor = jnp.minimum(1.0, math.sqrt(count) / (jnp.sqrt(squares) + 1e-06))
    last_ref[...] = grads.reshape(hidden, channels) * factor
    others = others * factor
    mid_ref[...] = others[:, :hidden]
    turned = others.T
    first_ref[...] = turned[hidden : hidden + order]
    first_bias_ref[...] = turned[hidden + order]
    mid_bias_ref[...] = turned[hidden + order + 1]


def on_device(inputs, grad_out, w_first, b_first, w_mid, b_mid, w_last, decay_rate):
    parts = lax.axis_size("ctx")
    groups = lax.axis_size("dp")
    channels = inputs.shape[2]
    hidden, order = w_first.shape
    own = channels // parts
    chunks = own // CC
    half = parts + 1
    seq = parts * FB
    rows = hidden // groups
    tables = make_tables(parts)
    vmem = pl.BlockSpec(memory_space=pltpu.VMEM)
    anywhere = pl.BlockSpec(memory_space=pl.ANY)
    last, small = pl.pallas_call(
        functools.partial(main_kernel, parts, groups),
        out_shape=(
            jax.ShapeDtypeStruct((groups, rows, channels), BF),
            jax.ShapeDtypeStruct((groups, rows, 128), F32),
        ),
        in_specs=[anywhere] * 9 + [vmem] * 5,
        out_specs=(vmem, vmem),
        scratch_shapes=[
            pltpu.VMEM((FB, channels), BF),
            pltpu.VMEM((FB, channels), BF),
            *(pltpu.VMEM(table.shape, table.dtype) for table in tables),
            pltpu.VMEM((hidden, 128), F32),
            pltpu.VMEM((parts, chunks, 2, CC, FB), BF),
            pltpu.VMEM((chunks, 2, parts * CC, FB), BF),
            pltpu.VMEM((half, 2, CC, 2 * FB), BF),
            pltpu.VMEM((2 * parts, CC, FB), BF),
            pltpu.VMEM((hidden, seq), F32),
            pltpu.VMEM((hidden, seq), BF),
            pltpu.VMEM((hidden, seq), F32),
            pltpu.VMEM((256, seq), BF),
            pltpu.VMEM((own, seq), F32),
            pltpu.VMEM((groups, 2 * rows, 128), F32),
            pltpu.VMEM((groups, 2 * rows, 128), F32),
            pltpu.VMEM((2 * rows, 128), F32),
            pltpu.VMEM((parts, 2 * rows, 128), F32),
            pltpu.VMEM((groups, rows, channels), BF),
            pltpu.VMEM((groups, rows, 128), F32),
            pltpu.SemaphoreType.DMA((9,)),
            pltpu.SemaphoreType.DMA((chunks,)),
            pltpu.SemaphoreType.DMA((chunks,)),
            pltpu.SemaphoreType.DMA((8,)),
        ],
        compiler_params=pltpu.CompilerParams(
            collective_id=0, has_side_effects=True, vmem_limit_bytes=60 * 1024 * 1024
        ),
    )(
        inputs[0], grad_out[0], *tables, w_last.T,
        w_first.T, b_first, w_mid, b_mid, decay_rate,
    )
    count = hidden * (order + hidden + 2) + channels * hidden
    first, first_bias, mid, mid_bias, last = pl.pallas_call(
        functools.partial(clip_kernel, count),
        out_shape=(
            jax.ShapeDtypeStruct((order, hidden), F32),
            jax.ShapeDtypeStruct((hidden,), F32),
            jax.ShapeDtypeStruct((hidden, hidden), F32),
            jax.ShapeDtypeStruct((hidden,), F32),
            jax.ShapeDtypeStruct((hidden, channels), F32),
        ),
        in_specs=[vmem] * 2,
        out_specs=(vmem,) * 5,
    )(last, small)
    return (first.T, first_bias, mid, mid_bias, last.T)


def solution(mesh):
    in_specs = (P("dp", "ctx", None), P("dp", "ctx", None), P(), P(), P(), P(), P(), P())
    out_specs = (P(), P(), P(), P(), P())
    return jax.shard_map(
        on_device, mesh=mesh, in_specs=in_specs, out_specs=out_specs, check_vma=False
    )
```

time: 107 us -> 89.5 us (0.84)
  local copies, waits for them, and re-layouts: 11.1 us -> 0 us
  Pallas kernels: 93 us -> 88.7 us
  other arithmetic: 1.48 us -> 0 us
    unnamed x7 -> x0, local copies, waits for them, and re-layouts: 4.54 us -> none
    pallas_call x2, Pallas kernels: 93 us -> 88.7 us  [the longest x1 86.6 us: on_device(): pl.pallas_call(functools.partial(main_kernel, parts, groups), out_shape=(...]
    broadcast_in_dim x4 -> x0, local copies, waits for them, and re-layouts: 4.23 us -> none  [the longest x2 1.52 us: on_device(): rates[:, None]]
    transpose x1 -> x0, other arithmetic: 1.48 us -> none  [on_device(): clip_last = (last.reshape(hidden, channels).astype(F32) * factor[0, 0]).T]
where the time goes in v3:
time: 89.5 us; the launch traced here: 89.3 us
  Pallas kernels  88.7 us (99%)
    pallas_call x1, Pallas kernels, on_device(): pl.pallas_call(functools.partial(main_kernel, parts, groups), out_shape=(...  86.6 us
    pallas_call x1, Pallas kernels, on_device(): pl.pallas_call(functools.partial(clip_kernel, count), out_shape=(jax.Shap...  2.07 us

profile of v3, /device:TPU:1, one launch (start us, length us, event | category | flops | bytes accessed | tf_op | source)
XLA Modules:
  0.0 89.3 jit_solution(8054831721884630629)
XLA Ops:
  0.6 86.6 %shard_map.173 = (bf16[8,8,2048]{2,1,0:T(8,128)(2,1)}, f32[8,8,128]{2,1,0:T(8,128)}) custom-call(bf16[256,2048]{1,0:T(8,128)(2,1)} %bitcast.6, bf16[256,2048]{1,0:T(8,128)(2,1)} %bitcast.7, bf16[1056,512]{1,0:T(8,128)(2,1)} %constant.12.clone.fwd_any, bf16[512,512]{1,0:T(8,128)(2,1)} %constant.13.clone.ef_any, bf16[512,512]{1,0:T(8,128)(2,1)} %constant.14.clone.ei_any, ...), custom_call_target="tpu_custom_call" | custom-call | tf_op jit(solution)/shard_map/pallas_call | solution.py:373
  87.2 2.1 %shard_map.174 = (f32[33,64]{1,0:T(8,128)}, f32[64]{0:T(128)}, f32[64,64]{1,0:T(8,128)}, f32[64]{0:T(128)}, f32[64,2048]{1,0:T(8,128)}) custom-call(bf16[8,8,2048]{2,1,0:T(8,128)(2,1)} %get-tuple-element.12.last_in, f32[8,8,128]{2,1,0:T(8,128)} %get-tuple-element.13.small_in), custom_call_target="tpu_custom_call" | custom-call | tf_op jit(solution)/shard_map/pallas_call | solution.py:414

commit v4 on v3

--- a/solution.py
+++ b/solution.py
@@ -18,6 +18,7 @@
 MESH = pl.DeviceIdType.MESH
 FP = 48
 SPAN = 2048
+NX = 4
 PI_HIGH = 1.570770263671875
 PI_LOW = math.pi / 2 - PI_HIGH
 
@@ -38,7 +39,8 @@
     ang = (f32(math.pi) * (j[:, None] * m[None, :] % (2 * seq)).astype(f32) / f32(seq)).astype(f32)
     tw = np.stack([np.cos(ang), -np.sin(ang)]).astype(f32)
     eye = np.eye(CC, dtype=f32)
-    forward = np.kron(np.concatenate([fr, fi], 0), eye).astype(bf)
+    by_x = n.reshape(rows // NX, NX).T.reshape(-1)
+    forward = np.kron(np.concatenate([fr, fi], 0)[:, by_x], eye).astype(bf)
     e_fwd = np.block([[er.T, ei.T], [-ei.T, er.T]]).astype(bf)
     e_inv = np.block([[er.T, -ei.T], [ei.T, er.T]]).astype(bf)
     twice = np.where(j % rows == 0, 1.0, 2.0).astype(f32)[:, None]
@@ -97,15 +99,25 @@
     )
 
 
+def ahead(place, step, count):
+    there = place + step
+    return jnp.where(there >= count, there - count, there)
+
+
+def behind(place, step, count):
+    there = place - step
+    return jnp.where(there < 0, there + count, there)
+
+
 def main_kernel(
     parts, groups,
     x_any, g_any, fwd_any, ef_any, ei_any, inv_any, tw_any, feats_any, wl_any,
     wf_ref, bf_ref, wm_ref, bm_ref, rate_ref,
     last_ref, small_ref,
     x_ref, g_ref, fwd_ref, ef_ref, ei_ref, inv_ref, tw_ref, feats_ref, wl_ref,
-    send, recv, spec, back, cos_first, act_second, cos_second, wide, modul,
-    part, got, own_part, ring, fin, small,
-    load_sem, send_sem, recv_sem, sems,
+    send, relay, recv, spec, back, cos_first, act_second, cos_second, wide, modul,
+    part, got, ring, column_last, column_small, fin, small,
+    load_sem, send_sem, relay_sem, recv_sem, sems,
 ):
     ctx = lax.axis_index("ctx")
     dp = lax.axis_index("dp")
@@ -130,62 +142,64 @@
     for load in loads:
         load.start()
 
+    nz = parts // NX
+    z, x = ctx // NX, lax.rem(ctx, NX)
+    round_x = [ahead(x, r, NX) for r in range(NX)]
+    round_z = [ahead(z, r, nz) for r in range(nz)]
+    round_dp = [ahead(dp, r, groups) for r in range(groups)]
+    peers_x = [{"ctx": z * NX + t} for t in round_x]
+    peers_z = [{"ctx": t * NX + x} for t in round_z]
+    peers_dp = [{"dp": t} for t in round_dp]
+
     barrier = pltpu.get_barrier_semaphore()
-
-    @pl.loop(1, parts)
-    def _(r):
-        pl.semaphore_signal(
-            barrier, inc=1, device_id={"ctx": lax.rem(ctx + r, parts)}, device_id_type=MESH
-        )
-
-    @pl.loop(1, groups)
-    def _(r):
-        pl.semaphore_signal(
-            barrier, inc=1, device_id={"dp": lax.rem(dp + r, groups)}, device_id_type=MESH
-        )
-
-    mine = pl.ds(pl.multiple_of(ctx * CC, CC), CC)
-
-    def copy_to(target, k):
-        return pltpu.make_async_remote_copy(
-            src_ref=send.at[target, k],
-            dst_ref=recv.at[k, :, mine],
-            send_sem=send_sem.at[k],
-            recv_sem=recv_sem.at[k],
-            device_id={"ctx": target},
-            device_id_type=MESH,
-        )
+    for peer in peers_z[1:] + peers_x[1:] + peers_dp[1:]:
+        pl.semaphore_signal(barrier, inc=1, device_id=peer, device_id_type=MESH)
 
     loads[0].wait()
     loads[1].wait()
-    pl.semaphore_wait(barrier, parts + groups - 2)
 
     @pl.loop(0, channels // 128)
-    def _(i):
-        e = lax.rem(ctx // pair + i + 1, channels // 128)
+    def _(e):
         lanes = pl.ds(pl.multiple_of(e * 128, 128), 128)
         for v, ref in enumerate((x_ref, g_ref)):
             turned = ref[:, lanes].T
             for a in range(pair):
+                to_z = (e * pair) // NX
+                to_x = lax.rem(e * pair, NX) + a
                 for k in range(chunks):
                     row = a * own + k * CC
-                    send[e * pair + a, k, v] = turned[row : row + CC]
-        for a in range(pair):
-
-            @pl.when(e * pair + a != ctx)
-            def _():
-                copy_to(e * pair + a, 0).start()
-
-    for k in range(1, chunks):
-
-        @pl.loop(0, parts - 1)
-        def _(i):
-            step = i // 2 + 1
-            r = jnp.where(lax.rem(i, 2) == 0, step, parts - step)
-            copy_to(lax.rem(ctx + r, parts), k).start()
+                    send[to_z, to_x, k, v] = turned[row : row + CC]
+
+    pl.semaphore_wait(barrier, nz + NX + groups - 3)
+
+    def start(source, target, first, second, peer):
+        pltpu.make_async_remote_copy(
+            src_ref=source, dst_ref=target, send_sem=first, recv_sem=second,
+            device_id=peer, device_id_type=MESH,
+        ).start()
 
     for k in range(chunks):
-        recv[k, :, mine] = send[ctx, k]
+        for r in range(1, NX):
+            start(
+                send.at[:, round_x[r], k], relay.at[k, :, :, NX - r], send_sem.at[k], relay_sem.at[k], peers_x[r]
+            )
+        for r in range(1, nz):
+            start(
+                send.at[round_z[r], x, k], recv.at[k, :, z, 0], send_sem.at[chunks + k], recv_sem.at[k], peers_z[r]
+            )
+
+    for k in range(chunks):
+        recv[k, :, z, 0] = send[z, x, k]
+
+    def forward(k):
+        landed = relay.at[k, :, :, 1:]
+        pltpu.make_async_copy(landed, landed, relay_sem.at[k]).wait()
+        for r in range(1, nz):
+            start(
+                relay.at[k, round_z[r], :, 1:], recv.at[k, :, z, 1:], send_sem.at[2 * chunks + k], recv_sem.at[k],
+                peers_z[r],
+            )
+        recv[k, :, z, 1:] = relay[k, z, :, 1:]
 
     for load in loads[2:]:
         load.wait()
@@ -207,8 +221,7 @@
     wide[128 : 128 + FP] = feats_ref[FP:]
     wide[128 + FP : top] = jnp.zeros((top - 128 - FP, seq), BF)
 
-    @pl.loop(0, seq // width)
-    def _(i):
+    def network(i):
         at = pl.ds(pl.multiple_of(i * width, width), width)
         high = feats_ref[:FP, at]
         stack = jnp.concatenate([high, feats_ref[FP:, at], high], axis=0)
@@ -224,16 +237,24 @@
         places = (i * width + lax.broadcasted_iota(jnp.int32, (1, width), 1)).astype(F32)
         modul[:, at] = jnp.exp(-(decay * places) / seq)
 
+    steps = seq // width
+    pl.loop(0, steps * 3 // 4)(network)
+    forward(0)
+    pl.loop(steps * 3 // 4, steps)(network)
+    for k in range(1, chunks):
+        forward(k)
+
     @pl.loop(0, chunks)
     def _(k):
-        for which in (send_sem, recv_sem):
-            pltpu.make_async_copy(
-                recv.at[k, :, : (parts - 1) * CC], recv.at[k, :, : (parts - 1) * CC], which.at[k]
-            ).wait()
+        landed = recv.at[k, :, : nz - 1]
+        pltpu.make_async_copy(landed, landed, recv_sem.at[k]).wait()
         turn_re = tw_ref[0][:, None, :]
         turn_im = tw_ref[1][:, None, :]
         for v in range(2):
-            part_all = mm(fwd_ref[...], recv[k, v])
+            columns = [
+                recv[k, v, :, behind(t, x, NX)].reshape(nz * CC, FB) for t in range(NX)
+            ]
+            part_all = mm(fwd_ref[...], jnp.concatenate(columns, axis=0))
             part_re = part_all[: half * CC].reshape(half, CC, FB)
             part_im = part_all[half * CC :].reshape(half, CC, FB)
             spec[:, v, :, :FB] = (part_re * turn_re - part_im * turn_im).astype(BF)
@@ -285,59 +306,58 @@
     part[:, :rows] = last.reshape(groups, rows, 128)
     part[:, rows:] = mixed.reshape(groups, rows, 128)
 
-    def wait(ref, first, second):
-        for which in (first, second):
-            pltpu.make_async_copy(ref, ref, sems.at[which]).wait()
-
-    @pl.loop(1, groups)
-    def _(r):
-        target = lax.rem(dp + r, groups)
-        pltpu.make_async_remote_copy(
-            src_ref=part.at[target], dst_ref=got.at[groups - r],
-            send_sem=sems.at[0], recv_sem=sems.at[1],
-            device_id={"dp": target}, device_id_type=MESH,
-        ).start()
-
-    wait(got.at[1:groups], 0, 1)
+    def wait(ref, which):
+        pltpu.make_async_copy(ref, ref, sems.at[which]).wait()
+
+    for r in range(1, groups):
+        start(part.at[round_dp[r]], got.at[groups - r], sems.at[0], sems.at[1], peers_dp[r])
+    wait(got.at[1:groups], 1)
     summed = part[dp]
     for r in range(1, groups):
         summed = summed + got[r]
-    own_part[...] = summed
     ring[0] = summed
 
-    @pl.loop(1, parts)
-    def _(r):
-        target = lax.rem(ctx + r, parts)
-        pltpu.make_async_remote_copy(
-            src_ref=own_part, dst_ref=ring.at[parts - r],
-            send_sem=sems.at[2], recv_sem=sems.at[3],
-            device_id={"ctx": target}, device_id_type=MESH,
-        ).start()
-
-    wait(ring.at[1:parts], 2, 3)
-    low_lanes = lax.broadcasted_iota(jnp.int32, (rows, 128), 1) < own
+    for r in range(1, nz):
+        start(ring.at[0], ring.at[nz - r], sems.at[2], sems.at[3], peers_z[r])
+    wait(ring.at[1:nz], 3)
     summed = jnp.zeros((rows, 128), F32)
-    for e in range(parts // 2):
-        one = ring[lax.rem(2 * e + parts - ctx, parts)]
-        two = ring[lax.rem(2 * e + 1 + parts - ctx, parts)]
-        fin[dp, :, 128 * e : 128 * (e + 1)] = jnp.where(low_lanes, one[:rows], two[:rows]).astype(BF)
-        summed = summed + one[rows:] + two[rows:]
-    small[dp] = summed
-
-    @pl.loop(1, groups)
-    def _(r):
-        target = lax.rem(dp + r, groups)
-        for ref, base in ((fin, 4), (small, 6)):
-            pltpu.make_async_remote_copy(
-                src_ref=ref.at[dp], dst_ref=ref.at[dp],
-                send_sem=sems.at[base], recv_sem=sems.at[base + 1],
-                device_id={"dp": target}, device_id_type=MESH,
-            ).start()
-
-    wait(fin.at[: groups - 1], 4, 5)
-    wait(small.at[: groups - 1], 6, 7)
+    for t in range(nz):
+        block = ring[behind(t, z, nz)]
+        column_last[0, t] = block[:rows].astype(BF)
+        summed = summed + block[rows:]
+    column_small[0] = summed
+
+    for r in range(1, NX):
+        start(column_last.at[0], column_last.at[NX - r], sems.at[4], sems.at[5], peers_x[r])
+        start(column_small.at[0], column_small.at[NX - r], sems.at[6], sems.at[7], peers_x[r])
+    wait(column_last.at[1:NX], 5)
+    wait(column_small.at[1:NX], 7)
+    small[dp] = jnp.sum(column_small[...], axis=0)
+    for t in range(0, NX, 2):
+        one = column_last[behind(t, x, NX)].astype(F32)
+        two = column_last[behind(t + 1, x, NX)].astype(F32)
+        both = jnp.where(lax.broadcasted_iota(jnp.int32, one.shape, 2) < own, one, two).astype(BF)
+        for i in range(nz):
+            at = (i * NX + t) // 2 * 128
+            fin[dp, :, at : at + 128] = both[i]
+
+    for r in range(1, groups):
+        start(fin.at[dp], fin.at[dp], sems.at[8], sems.at[9], peers_dp[r])
+        start(small.at[dp], small.at[dp], sems.at[10], sems.at[11], peers_dp[r])
+    wait(fin.at[: groups - 1], 9)
+    wait(small.at[: groups - 1], 11)
     last_ref[...] = fin[...]
     small_ref[...] = small[...]
+
+    wait(got.at[1:groups], 0)
+    wait(ring.at[1:nz], 2)
+    wait(column_last.at[1:NX], 4)
+    wait(column_small.at[1:NX], 6)
+    wait(fin.at[: groups - 1], 8)
+    wait(small.at[: groups - 1], 10)
+    for k in range(chunks):
+        for i, ref in enumerate((relay.at[k, :, :, 1:], recv.at[k, :, : nz - 1, 0], recv.at[k, :, : nz - 1, 1:])):
+            pltpu.make_async_copy(ref, ref, send_sem.at[i * chunks + k]).wait()
 
 
 def clip_kernel(count, last_in, small_in, first_ref, first_bias_ref, mid_ref, mid_bias_ref, last_ref):
@@ -367,6 +387,7 @@
     half = parts + 1
     seq = parts * FB
     rows = hidden // groups
+    nz = parts // NX
     tables = make_tables(parts)
     vmem = pl.BlockSpec(memory_space=pltpu.VMEM)
     anywhere = pl.BlockSpec(memory_space=pl.ANY)
@@ -383,8 +404,9 @@
             pltpu.VMEM((FB, channels), BF),
             *(pltpu.VMEM(table.shape, table.dtype) for table in tables),
             pltpu.VMEM((hidden, 128), F32),
-            pltpu.VMEM((parts, chunks, 2, CC, FB), BF),
-            pltpu.VMEM((chunks, 2, parts * CC, FB), BF),
+            pltpu.VMEM((nz, NX, chunks, 2, CC, FB), BF),
+            pltpu.VMEM((chunks, nz, 2, NX, CC, FB), BF),
+            pltpu.VMEM((chunks, 2, nz, NX, CC, FB), BF),
             pltpu.VMEM((half, 2, CC, 2 * FB), BF),
             pltpu.VMEM((2 * parts, CC, FB), BF),
             pltpu.VMEM((hidden, seq), F32),
@@ -394,14 +416,16 @@
             pltpu.VMEM((own, seq), F32),
             pltpu.VMEM((groups, 2 * rows, 128), F32),
             pltpu.VMEM((groups, 2 * rows, 128), F32),
-            pltpu.VMEM((2 * rows, 128), F32),
-            pltpu.VMEM((parts, 2 * rows, 128), F32),
+            pltpu.VMEM((nz, 2 * rows, 128), F32),
+            pltpu.VMEM((NX, nz, rows, 128), BF),
+            pltpu.VMEM((NX, rows, 128), F32),
             pltpu.VMEM((groups, rows, channels), BF),
             pltpu.VMEM((groups, rows, 128), F32),
             pltpu.SemaphoreType.DMA((9,)),
+            pltpu.SemaphoreType.DMA((3 * chunks,)),
             pltpu.SemaphoreType.DMA((chunks,)),
             pltpu.SemaphoreType.DMA((chunks,)),
-            pltpu.SemaphoreType.DMA((8,)),
+            pltpu.SemaphoreType.DMA((12,)),
         ],
         compiler_params=pltpu.CompilerParams(
             collective_id=0, has_side_effects=True, vmem_limit_bytes=60 * 1024 * 1024

time: 89.5 us -> 85.2 us (0.952)
  Pallas kernels: 88.7 us -> 84.4 us
    pallas_call x1, Pallas kernels: 86.6 us -> 82.3 us  [on_device(): pl.pallas_call(functools.partial(main_kernel, parts, groups), out_shape=(...]
where the time goes in v4:
time: 85.2 us; the launch traced here: 85 us
  Pallas kernels  84.4 us (99%)
    pallas_call x1, Pallas kernels, on_device(): pl.pallas_call(functools.partial(main_kernel, parts, groups), out_shape=(...  82.3 us
    pallas_call x1, Pallas kernels, on_device(): pl.pallas_call(functools.partial(clip_kernel, count), out_shape=(jax.Shap...  2.07 us

profile of v4, /device:TPU:1, one launch (start us, length us, event | category | flops | bytes accessed | tf_op | source)
XLA Modules:
  0.0 85.0 jit_solution(7031102749566318184)
XLA Ops:
  0.6 82.3 %shard_map.173 = (bf16[8,8,2048]{2,1,0:T(8,128)(2,1)}, f32[8,8,128]{2,1,0:T(8,128)}) custom-call(bf16[256,2048]{1,0:T(8,128)(2,1)} %bitcast.6, bf16[256,2048]{1,0:T(8,128)(2,1)} %bitcast.7, bf16[1056,512]{1,0:T(8,128)(2,1)} %constant.12.clone.fwd_any, bf16[512,512]{1,0:T(8,128)(2,1)} %constant.13.clone.ef_any, bf16[512,512]{1,0:T(8,128)(2,1)} %constant.14.clone.ei_any, ...), custom_call_target="tpu_custom_call" | custom-call | tf_op jit(solution)/shard_map/pallas_call | solution.py:394
  83.0 2.1 %shard_map.174 = (f32[33,64]{1,0:T(8,128)}, f32[64]{0:T(128)}, f32[64,64]{1,0:T(8,128)}, f32[64]{0:T(128)}, f32[64,2048]{1,0:T(8,128)}) custom-call(bf16[8,8,2048]{2,1,0:T(8,128)(2,1)} %get-tuple-element.12.last_in, f32[8,8,128]{2,1,0:T(8,128)} %get-tuple-element.13.small_in), custom_call_target="tpu_custom_call" | custom-call | tf_op jit(solution)/shard_map/pallas_call | solution.py:438

commit v5 on v4

--- a/solution.py
+++ b/solution.py
@@ -116,7 +116,7 @@
     last_ref, small_ref,
     x_ref, g_ref, fwd_ref, ef_ref, ei_ref, inv_ref, tw_ref, feats_ref, wl_ref,
     send, relay, recv, spec, back, cos_first, act_second, cos_second, wide, modul,
-    part, got, ring, column_last, column_small, fin, small,
+    part, got, ring, fin, small,
     load_sem, send_sem, relay_sem, recv_sem, sems,
 ):
     ctx = lax.axis_index("ctx")
@@ -244,8 +244,7 @@
     for k in range(1, chunks):
         forward(k)
 
-    @pl.loop(0, chunks)
-    def _(k):
+    def transform(k):
         landed = recv.at[k, :, : nz - 1]
         pltpu.make_async_copy(landed, landed, recv_sem.at[k]).wait()
         turn_re = tw_ref[0][:, None, :]
@@ -270,12 +269,15 @@
         back[:half] = (in_re * turn_re + in_im * turn_im).astype(BF)
         back[half:] = (in_im * turn_re - in_re * turn_im)[1:parts].astype(BF)
         grad = mm(inv_ref[...], back[...].reshape(2 * parts * CC, FB))
-        first_row = pl.multiple_of(k * CC, CC)
+        first_row = k * CC if isinstance(k, int) else pl.multiple_of(k * CC, CC)
         for s in range(parts):
             at = slice(s * FB, (s + 1) * FB)
             wide[pl.ds(top + first_row, CC), at] = (
                 grad[s * CC : (s + 1) * CC] * modul[pl.ds(first_row, CC), at]
             ).astype(BF)
+
+    pl.loop(0, chunks - 1)(transform)
+    transform(chunks - 1)
 
     span = SPAN
     tile = jnp.where(odd, pltpu.roll(wl_ref[...], own, 1), wl_ref[...])[:, :own]
@@ -315,46 +317,32 @@
     summed = part[dp]
     for r in range(1, groups):
         summed = summed + got[r]
-    ring[0] = summed
-
-    for r in range(1, nz):
-        start(ring.at[0], ring.at[nz - r], sems.at[2], sems.at[3], peers_z[r])
-    wait(ring.at[1:nz], 3)
+    ring[0] = summed.astype(BF)
+
+    for r in range(1, parts):
+        start(ring.at[0], ring.at[parts - r], sems.at[2], sems.at[3], {"ctx": ahead(ctx, r, parts)})
+    wait(ring.at[1:parts], 3)
+    low_lanes = lax.broadcasted_iota(jnp.int32, (rows, 128), 1) < own
     summed = jnp.zeros((rows, 128), F32)
-    for t in range(nz):
-        block = ring[behind(t, z, nz)]
-        column_last[0, t] = block[:rows].astype(BF)
-        summed = summed + block[rows:]
-    column_small[0] = summed
-
-    for r in range(1, NX):
-        start(column_last.at[0], column_last.at[NX - r], sems.at[4], sems.at[5], peers_x[r])
-        start(column_small.at[0], column_small.at[NX - r], sems.at[6], sems.at[7], peers_x[r])
-    wait(column_last.at[1:NX], 5)
-    wait(column_small.at[1:NX], 7)
-    small[dp] = jnp.sum(column_small[...], axis=0)
-    for t in range(0, NX, 2):
-        one = column_last[behind(t, x, NX)].astype(F32)
-        two = column_last[behind(t + 1, x, NX)].astype(F32)
-        both = jnp.where(lax.broadcasted_iota(jnp.int32, one.shape, 2) < own, one, two).astype(BF)
-        for i in range(nz):
-            at = (i * NX + t) // 2 * 128
-            fin[dp, :, at : at + 128] = both[i]
+    for t in range(0, parts, 2):
+        one = ring[behind(t, ctx, parts)].astype(F32)
+        two = ring[behind(t + 1, ctx, parts)].astype(F32)
+        fin[dp, :, t * own : t * own + 128] = jnp.where(low_lanes, one[:rows], two[:rows]).astype(BF)
+        summed = summed + (one[rows:] + two[rows:])
+    small[dp] = summed
 
     for r in range(1, groups):
-        start(fin.at[dp], fin.at[dp], sems.at[8], sems.at[9], peers_dp[r])
-        start(small.at[dp], small.at[dp], sems.at[10], sems.at[11], peers_dp[r])
-    wait(fin.at[: groups - 1], 9)
-    wait(small.at[: groups - 1], 11)
+        start(fin.at[dp], fin.at[dp], sems.at[4], sems.at[5], peers_dp[r])
+        start(small.at[dp], small.at[dp], sems.at[6], sems.at[7], peers_dp[r])
+    wait(fin.at[: groups - 1], 5)
+    wait(small.at[: groups - 1], 7)
     last_ref[...] = fin[...]
     small_ref[...] = small[...]
 
     wait(got.at[1:groups], 0)
-    wait(ring.at[1:nz], 2)
-    wait(column_last.at[1:NX], 4)
-    wait(column_small.at[1:NX], 6)
-    wait(fin.at[: groups - 1], 8)
-    wait(small.at[: groups - 1], 10)
+    wait(ring.at[1:parts], 2)
+    wait(fin.at[: groups - 1], 4)
+    wait(small.at[: groups - 1], 6)
     for k in range(chunks):
         for i, ref in enumerate((relay.at[k, :, :, 1:], recv.at[k, :, : nz - 1, 0], recv.at[k, :, : nz - 1, 1:])):
             pltpu.make_async_copy(ref, ref, send_sem.at[i * chunks + k]).wait()
@@ -416,16 +404,14 @@
             pltpu.VMEM((own, seq), F32),
             pltpu.VMEM((groups, 2 * rows, 128), F32),
             pltpu.VMEM((groups, 2 * rows, 128), F32),
-            pltpu.VMEM((nz, 2 * rows, 128), F32),
-            pltpu.VMEM((NX, nz, rows, 128), BF),
-            pltpu.VMEM((NX, rows, 128), F32),
+            pltpu.VMEM((parts, 2 * rows, 128), BF),
             pltpu.VMEM((groups, rows, channels), BF),
             pltpu.VMEM((groups, rows, 128), F32),
             pltpu.SemaphoreType.DMA((9,)),
             pltpu.SemaphoreType.DMA((3 * chunks,)),
             pltpu.SemaphoreType.DMA((chunks,)),
             pltpu.SemaphoreType.DMA((chunks,)),
-            pltpu.SemaphoreType.DMA((12,)),
+            pltpu.SemaphoreType.DMA((8,)),
         ],
         compiler_params=pltpu.CompilerParams(
             collective_id=0, has_side_effects=True, vmem_limit_bytes=60 * 1024 * 1024

time: 85.2 us -> 83.8 us (0.984)
  Pallas kernels: 84.4 us -> 83 us
    pallas_call x1, Pallas kernels: 82.3 us -> 81 us  [on_device(): pl.pallas_call(functools.partial(main_kernel, parts, groups), out_shape=(...]
where the time goes in v5:
time: 83.8 us; the launch traced here: 83.7 us
  Pallas kernels  83 us (99%)
    pallas_call x1, Pallas kernels, on_device(): pl.pallas_call(functools.partial(main_kernel, parts, groups), out_shape=(...  81 us
    pallas_call x1, Pallas kernels, on_device(): pl.pallas_call(functools.partial(clip_kernel, count), out_shape=(jax.Shap...  2.07 us

profile of v5, /device:TPU:1, one launch (start us, length us, event | category | flops | bytes accessed | tf_op | source)
XLA Modules:
  0.0 83.7 jit_solution(16916306242732423555)
XLA Ops:
  0.6 81.0 %shard_map.173 = (bf16[8,8,2048]{2,1,0:T(8,128)(2,1)}, f32[8,8,128]{2,1,0:T(8,128)}) custom-call(bf16[256,2048]{1,0:T(8,128)(2,1)} %bitcast.6, bf16[256,2048]{1,0:T(8,128)(2,1)} %bitcast.7, bf16[1056,512]{1,0:T(8,128)(2,1)} %constant.12.clone.fwd_any, bf16[512,512]{1,0:T(8,128)(2,1)} %constant.13.clone.ef_any, bf16[512,512]{1,0:T(8,128)(2,1)} %constant.14.clone.ei_any, ...), custom_call_target="tpu_custom_call" | custom-call | tf_op jit(solution)/shard_map/pallas_call | solution.py:382
  81.6 2.1 %shard_map.174 = (f32[33,64]{1,0:T(8,128)}, f32[64]{0:T(128)}, f32[64,64]{1,0:T(8,128)}, f32[64]{0:T(128)}, f32[64,2048]{1,0:T(8,128)}) custom-call(bf16[8,8,2048]{2,1,0:T(8,128)(2,1)} %get-tuple-element.12.last_in, f32[8,8,128]{2,1,0:T(8,128)} %get-tuple-element.13.small_in), custom_call_target="tpu_custom_call" | custom-call | tf_op jit(solution)/shard_map/pallas_call | solution.py:424

commit v6 on v5

--- a/solution.py
+++ b/solution.py
@@ -18,6 +18,7 @@
 MESH = pl.DeviceIdType.MESH
 FP = 48
 SPAN = 2048
+HALVES = 2
 NX = 4
 PI_HIGH = 1.570770263671875
 PI_LOW = math.pi / 2 - PI_HIGH
@@ -112,12 +113,13 @@
 def main_kernel(
     parts, groups,
     x_any, g_any, fwd_any, ef_any, ei_any, inv_any, tw_any, feats_any, wl_any,
-    wf_ref, bf_ref, wm_ref, bm_ref, rate_ref,
+    wf_any, bf_any, wm_any, bm_any, rate_any,
     last_ref, small_ref,
     x_ref, g_ref, fwd_ref, ef_ref, ei_ref, inv_ref, tw_ref, feats_ref, wl_ref,
+    wf_ref, bf_ref, wm_ref, bm_ref, rate_ref,
     send, relay, recv, spec, back, cos_first, act_second, cos_second, wide, modul,
     part, got, ring, fin, small,
-    load_sem, send_sem, relay_sem, recv_sem, sems,
+    block_sem, load_sem, send_sem, relay_sem, recv_sem, sems,
 ):
     ctx = lax.axis_index("ctx")
     dp = lax.axis_index("dp")
@@ -130,16 +132,23 @@
     pair = 128 // own
 
     lanes_own = pl.ds(pl.multiple_of((ctx // pair) * 128, 128), 128)
+    parted = [pl.ds(i * (channels // HALVES), channels // HALVES) for i in range(HALVES)]
+    blocks = [
+        pltpu.make_async_copy(source.at[:, at], target.at[:, at], block_sem.at[2 * i + v])
+        for i, at in enumerate(parted)
+        for v, (source, target) in enumerate(((x_any, x_ref), (g_any, g_ref)))
+    ]
     loads = [
         pltpu.make_async_copy(source, target, load_sem.at[i])
         for i, (source, target) in enumerate(
             (
-                (x_any, x_ref), (g_any, g_ref), (wl_any.at[:, lanes_own], wl_ref), (feats_any, feats_ref),
-                (tw_any, tw_ref), (fwd_any, fwd_ref), (ef_any, ef_ref), (ei_any, ei_ref), (inv_any, inv_ref),
+                (wf_any, wf_ref), (bf_any, bf_ref), (wm_any, wm_ref), (bm_any, bm_ref), (rate_any, rate_ref),
+                (wl_any.at[:, lanes_own], wl_ref), (feats_any, feats_ref), (tw_any, tw_ref),
+                (fwd_any, fwd_ref), (ef_any, ef_ref), (ei_any, ei_ref), (inv_any, inv_ref),
             )
         )
     ]
-    for load in loads:
+    for load in blocks:
         load.start()
 
     nz = parts // NX
@@ -152,14 +161,13 @@
     peers_dp = [{"dp": t} for t in round_dp]
 
     barrier = pltpu.get_barrier_semaphore()
-    for peer in peers_z[1:] + peers_x[1:] + peers_dp[1:]:
+    far_z = sorted(range(1, nz), key=lambda r: -min(r, nz - r))
+    for peer in [peers_z[r] for r in far_z] + peers_x[1:] + peers_dp[1:]:
         pl.semaphore_signal(barrier, inc=1, device_id=peer, device_id_type=MESH)
-
-    loads[0].wait()
-    loads[1].wait()
-
-    @pl.loop(0, channels // 128)
-    def _(e):
+    for load in loads:
+        load.start()
+
+    def turn(e):
         lanes = pl.ds(pl.multiple_of(e * 128, 128), 128)
         for v, ref in enumerate((x_ref, g_ref)):
             turned = ref[:, lanes].T
@@ -170,6 +178,12 @@
                     row = a * own + k * CC
                     send[to_z, to_x, k, v] = turned[row : row + CC]
 
+    tiles = channels // 128 // HALVES
+    for i in range(HALVES):
+        blocks[2 * i].wait()
+        blocks[2 * i + 1].wait()
+        pl.loop(i * tiles, (i + 1) * tiles)(turn)
+
     pl.semaphore_wait(barrier, nz + NX + groups - 3)
 
     def start(source, target, first, second, peer):
@@ -201,7 +215,7 @@
             )
         recv[k, :, z, 1:] = relay[k, z, :, 1:]
 
-    for load in loads[2:]:
+    for load in loads:
         load.wait()
     width = 512
     top = 256 - own
@@ -385,13 +399,18 @@
             jax.ShapeDtypeStruct((groups, rows, channels), BF),
             jax.ShapeDtypeStruct((groups, rows, 128), F32),
         ),
-        in_specs=[anywhere] * 9 + [vmem] * 5,
+        in_specs=[anywhere] * 14,
         out_specs=(vmem, vmem),
         scratch_shapes=[
             pltpu.VMEM((FB, channels), BF),
             pltpu.VMEM((FB, channels), BF),
             *(pltpu.VMEM(table.shape, table.dtype) for table in tables),
             pltpu.VMEM((hidden, 128), F32),
+            pltpu.VMEM((order, hidden), F32),
+            pltpu.VMEM((hidden,), F32),
+            pltpu.VMEM((hidden, hidden), F32),
+            pltpu.VMEM((hidden,), F32),
+            pltpu.VMEM((channels,), F32),
             pltpu.VMEM((nz, NX, chunks, 2, CC, FB), BF),
             pltpu.VMEM((chunks, nz, 2, NX, CC, FB), BF),
             pltpu.VMEM((chunks, 2, nz, NX, CC, FB), BF),
@@ -407,7 +426,8 @@
             pltpu.VMEM((parts, 2 * rows, 128), BF),
             pltpu.VMEM((groups, rows, channels), BF),
             pltpu.VMEM((groups, rows, 128), F32),
-            pltpu.SemaphoreType.DMA((9,)),
+            pltpu.SemaphoreType.DMA((2 * HALVES,)),
+            pltpu.SemaphoreType.DMA((12,)),
             pltpu.SemaphoreType.DMA((3 * chunks,)),
             pltpu.SemaphoreType.DMA((chunks,)),
             pltpu.SemaphoreType.DMA((chunks,)),

time: 83.8 us -> 82.9 us (0.989)
  Pallas kernels: 83 us -> 82.1 us
    pallas_call x1, Pallas kernels: 81 us -> 80.1 us  [on_device(): pl.pallas_call(functools.partial(main_kernel, parts, groups), out_shape=(...]
where the time goes in v6:
time: 82.9 us; the launch traced here: 82.8 us
  Pallas kernels  82.1 us (99%)
    pallas_call x1, Pallas kernels, on_device(): pl.pallas_call(functools.partial(main_kernel, parts, groups), out_shape=(...  80.1 us
    pallas_call x1, Pallas kernels, on_device(): pl.pallas_call(functools.partial(clip_kernel, count), out_shape=(jax.Shap...  2.07 us

profile of v6, /device:TPU:1, one launch (start us, length us, event | category | flops | bytes accessed | tf_op | source)
XLA Modules:
  0.0 82.8 jit_solution(16193034327441893331)
XLA Ops:
  0.6 80.1 %shard_map.173 = (bf16[8,8,2048]{2,1,0:T(8,128)(2,1)}, f32[8,8,128]{2,1,0:T(8,128)}) custom-call(bf16[256,2048]{1,0:T(8,128)(2,1)} %bitcast.6, bf16[256,2048]{1,0:T(8,128)(2,1)} %bitcast.7, bf16[1056,512]{1,0:T(8,128)(2,1)} %constant.12.clone.fwd_any, bf16[512,512]{1,0:T(8,128)(2,1)} %constant.13.clone.ef_any, bf16[512,512]{1,0:T(8,128)(2,1)} %constant.14.clone.ei_any, ...), custom_call_target="tpu_custom_call" | custom-call | tf_op jit(solution)/shard_map/pallas_call | solution.py:396
  80.7 2.1 %shard_map.174 = (f32[33,64]{1,0:T(8,128)}, f32[64]{0:T(128)}, f32[64,64]{1,0:T(8,128)}, f32[64]{0:T(128)}, f32[64,2048]{1,0:T(8,128)}) custom-call(bf16[8,8,2048]{2,1,0:T(8,128)(2,1)} %get-tuple-element.12.last_in, f32[8,8,128]{2,1,0:T(8,128)} %get-tuple-element.13.small_in), custom_call_target="tpu_custom_call" | custom-call | tf_op jit(solution)/shard_map/pallas_call | solution.py:444

commit v7 on v6

--- a/solution.py
+++ b/solution.py
@@ -119,7 +119,7 @@
     wf_ref, bf_ref, wm_ref, bm_ref, rate_ref,
     send, relay, recv, spec, back, cos_first, act_second, cos_second, wide, modul,
     part, got, ring, fin, small,
-    block_sem, load_sem, send_sem, relay_sem, recv_sem, sems,
+    block_sem, load_sem, send_sem, relay_sem, recv_sem, sems, result_sem,
 ):
     ctx = lax.axis_index("ctx")
     dp = lax.axis_index("dp")
@@ -350,8 +350,12 @@
         start(small.at[dp], small.at[dp], sems.at[6], sems.at[7], peers_dp[r])
     wait(fin.at[: groups - 1], 5)
     wait(small.at[: groups - 1], 7)
-    last_ref[...] = fin[...]
-    small_ref[...] = small[...]
+    results = [
+        pltpu.make_async_copy(source, target, result_sem.at[i])
+        for i, (source, target) in enumerate(((fin, last_ref), (small, small_ref)))
+    ]
+    for result in results:
+        result.start()
 
     wait(got.at[1:groups], 0)
     wait(ring.at[1:parts], 2)
@@ -360,6 +364,8 @@
     for k in range(chunks):
         for i, ref in enumerate((relay.at[k, :, :, 1:], recv.at[k, :, : nz - 1, 0], recv.at[k, :, : nz - 1, 1:])):
             pltpu.make_async_copy(ref, ref, send_sem.at[i * chunks + k]).wait()
+    for result in results:
+        result.wait()
 
 
 def clip_kernel(count, last_in, small_in, first_ref, first_bias_ref, mid_ref, mid_bias_ref, last_ref):
@@ -400,7 +406,7 @@
             jax.ShapeDtypeStruct((groups, rows, 128), F32),
         ),
         in_specs=[anywhere] * 14,
-        out_specs=(vmem, vmem),
+        out_specs=(anywhere, anywhere),
         scratch_shapes=[
             pltpu.VMEM((FB, channels), BF),
             pltpu.VMEM((FB, channels), BF),
@@ -432,6 +438,7 @@
             pltpu.SemaphoreType.DMA((chunks,)),
             pltpu.SemaphoreType.DMA((chunks,)),
             pltpu.SemaphoreType.DMA((8,)),
+            pltpu.SemaphoreType.DMA((2,)),
         ],
         compiler_params=pltpu.CompilerParams(
             collective_id=0, has_side_effects=True, vmem_limit_bytes=60 * 1024 * 1024

time: 82.9 us -> 82.8 us (level)
  no operation moved by 1% of the time
where the time goes in v7:
time: 82.8 us; the launch traced here: 82.7 us
  Pallas kernels  82.1 us (99%)
    pallas_call x1, Pallas kernels, on_device(): pl.pallas_call(functools.partial(main_kernel, parts, groups), out_shape=(...  80 us
    pallas_call x1, Pallas kernels, on_device(): pl.pallas_call(functools.partial(clip_kernel, count), out_shape=(jax.Shap...  2.07 us

profile of v7, /device:TPU:1, one launch (start us, length us, event | category | flops | bytes accessed | tf_op | source)
XLA Modules:
  0.0 82.7 jit_solution(14942467656236764525)
XLA Ops:
  0.6 80.0 %shard_map.173 = (bf16[8,8,2048]{2,1,0:T(8,128)(2,1)}, f32[8,8,128]{2,1,0:T(8,128)}) custom-call(bf16[256,2048]{1,0:T(8,128)(2,1)} %bitcast.6, bf16[256,2048]{1,0:T(8,128)(2,1)} %bitcast.7, bf16[1056,512]{1,0:T(8,128)(2,1)} %constant.12.clone.fwd_any, bf16[512,512]{1,0:T(8,128)(2,1)} %constant.13.clone.ef_any, bf16[512,512]{1,0:T(8,128)(2,1)} %constant.14.clone.ei_any, ...), custom_call_target="tpu_custom_call" | custom-call | tf_op jit(solution)/shard_map/pallas_call | solution.py:402
  80.7 2.1 %shard_map.174 = (f32[33,64]{1,0:T(8,128)}, f32[64]{0:T(128)}, f32[64,64]{1,0:T(8,128)}, f32[64]{0:T(128)}, f32[64,2048]{1,0:T(8,128)}) custom-call(bf16[8,8,2048]{2,1,0:T(8,128)(2,1)} %get-tuple-element.12.last_in, f32[8,8,128]{2,1,0:T(8,128)} %get-tuple-element.13.small_in), custom_call_target="tpu_custom_call" | custom-call | tf_op jit(solution)/shard_map/pallas_call | solution.py:451
